TPU v7x, 256 devices: a whole 4x4x8 slice. The times are simulated.
256 devices in a mesh: cp: 64 (over y, z, core), hd: 4 (over x).
Axes of the slice: x: 4, y: 4, z: 8, core: 2. Of those that a mesh axis runs over, the one named last changes fastest.
Arguments:
- query_projection: bfloat16 [32768, 8192], P(('cp', 'hd')), may hold values from -8 to 8
- key_projection: bfloat16 [32768, 1024], P(('cp', 'hd')), may hold values from -8 to 8
- value_projection: bfloat16 [32768, 1024], P(('cp', 'hd')), may hold values from -6 to 6
- output_gradient: bfloat16 [32768, 8192], P(('cp', 'hd')), may hold values from -6 to 6
- doc_ids: int32 [32768], replicated, may hold values from 0 to 127, never falling along the last dimension, each value on 1 to 512 neighbouring positions
- tile_plan: int32 [64], replicated, may hold values from 0 to 2, as said below
Outputs:
- query_grad: bfloat16 [32768, 8192], P('cp', 'hd')
- key_gradient: bfloat16 [32768, 1024], P('cp', 'hd')
- value_gradient: bfloat16 [32768, 1024], P('cp', 'hd')
Inputs may be any that keep to these rules, and one draw needn't show every extreme that they name: `doc_ids`: document ids never fall; every document has at most 512 tokens, and one has exactly 512. `tile_plan`: entry 0 and entry 62 are 0; entry 1 and the last entry are 2; where an entry is 2, the entry before it is 0.
All inputs are finite; a program needn't handle non-finite values.
Results may differ from a plain program's by a relative error of at most 0.007.
Values may be sent and summed in bfloat16 or wider, within the bound.
No kernel may reach another device: no remote copies, remote signals or barrier semaphores. Data moves between devices by JAX's collectives and lax.ppermute only.
A program may use at most 256 MiB of HBM per device.

v0:
```python
import functools
import math

import jax
import jax.numpy as jnp
from jax import lax
from jax.experimental import pallas as pl
from jax.experimental.pallas import tpu as pltpu
from jax.sharding import PartitionSpec as P

HEAD_DIM = 128
TILE = 128
STACK = 4
SHIFTS = (1, -1, 2)
PARTS = ((0, 0, 8), (1, 0, 4), (1, 4, 4))

ANY = pl.BlockSpec(memory_space=pl.ANY)
VMEM = pl.BlockSpec(memory_space=pltpu.VMEM)
SMEM = pl.BlockSpec(memory_space=pltpu.SMEM)
ROWS_BY_ROWS = (((1,), (1,)), ((), ()))
ROWS_BY_COLUMNS = (((1,), (0,)), ((), ()))


def dot(left, right, dims):
    return lax.dot_general(left, right, dims, preferred_element_type=jnp.float32)


def aligned(index, unit):
    return pl.multiple_of(index * unit, unit)


def source_of(me, shift):
    return lax.rem(me - shift + 4, 4)


def run_copies(pairs, staging, sems):
    ins = [
        pltpu.make_async_copy(src, staging.at[i], sems.at[0, i]) for i, (src, _) in enumerate(pairs)
    ]
    outs = [
        pltpu.make_async_copy(staging.at[i], dst, sems.at[1, i]) for i, (_, dst) in enumerate(pairs)
    ]
    for copy in ins:
        copy.start()
    for i, copy in enumerate(ins):
        copy.wait()
        outs[i].start()
    for copy in outs:
        copy.wait()


def cut_pairs(me, pieces, outs):
    pairs = []
    for shift, out in zip(SHIFTS, outs):
        to = lax.rem(me + shift + 4, 4)
        for at, (array, share, first, width) in enumerate(pieces):
            column = pl.multiple_of(to * share + first, TILE)
            pairs.append((array.at[:, pl.ds(column, width)], out.at[at]))
    return pairs


def cut_kernel(shares, me_ref, left, right, out_a, out_b, out_c, staging, sems):
    pieces = [(array, *shares) for array in (left, right)]
    run_copies(cut_pairs(me_ref[0], pieces, (out_a, out_b, out_c)), staging, sems)


def cut(me, left, right, share, first, width):
    rows = left.shape[0]
    shape = jax.ShapeDtypeStruct((2, rows, width), left.dtype)
    return pl.pallas_call(
        functools.partial(cut_kernel, (share, first, width)),
        out_shape=(shape,) * 3,
        in_specs=[SMEM, ANY, ANY],
        out_specs=(ANY,) * 3,
        scratch_shapes=[
            pltpu.VMEM((6, rows, width), left.dtype),
            pltpu.SemaphoreType.DMA((2, 6)),
        ],
        cost_estimate=pl.CostEstimate(
            flops=0, bytes_accessed=12 * rows * width * 2, transcendentals=0
        ),
    )(me, left, right)


def join_kernel(width, me_ref, got_a, got_b, got_c, left, right, out, staging, sems):
    me = me_ref[0]
    rows = left.shape[0]
    pairs = []
    for shift, got in zip(SHIFTS, (got_a, got_b, got_c)):
        at = pl.ds(aligned(source_of(me, shift), rows), rows)
        pairs += [(got.at[i], out.at[i, at, :]) for i in range(2)]
    at = pl.ds(aligned(me, rows), rows)
    columns = pl.ds(aligned(me, width), width)
    pairs += [(array.at[:, columns], out.at[i, at, :]) for i, array in enumerate((left, right))]
    run_copies(pairs, staging, sems)


def join(me, got, left, right):
    rows, width = got[0].shape[1:]
    return pl.pallas_call(
        functools.partial(join_kernel, width),
        out_shape=jax.ShapeDtypeStruct((2, 4 * rows, width), left.dtype),
        in_specs=[SMEM] + [ANY] * 5,
        out_specs=ANY,
        scratch_shapes=[
            pltpu.VMEM((8, rows, width), left.dtype),
            pltpu.SemaphoreType.DMA((2, 8)),
        ],
        cost_estimate=pl.CostEstimate(
            flops=0, bytes_accessed=16 * rows * width * 2, transcendentals=0
        ),
    )(me, *got, left, right)


def attention_kernel(part, has_query, has_sums, ends, *refs):
    group, first, heads = part
    stacks = heads // STACK
    wide = STACK * HEAD_DIM
    refs = list(refs)
    scal, start, kv_own, kv_prev, got_a, got_b, got_c, query, dout = refs[:9]
    refs = refs[9 + has_query :]
    if has_sums:
        sums_in = refs.pop(0)
    query_out = refs.pop(0)
    if ends:
        own_out, prior_out = refs.pop(0), refs.pop(0)
    else:
        sums_out = refs.pop(0)
    q_all, d_all, keys, values, keys_t, bias, sums, dq, kv_sems, in_sems, out_sems = refs
    me = scal[0]
    rows = query.shape[0]
    block = 4 * rows

    kv_copies = []
    for i, target in enumerate((keys, values)):
        for j, source in enumerate((kv_prev, kv_own)):
            kv_copies.append(
                pltpu.make_async_copy(
                    source.at[i, :, pl.ds(group * HEAD_DIM, HEAD_DIM)],
                    target.at[pl.ds(j * block, block), :],
                    kv_sems.at[2 * i + j],
                )
            )
    if has_sums:
        kv_copies.append(pltpu.make_async_copy(sums_in, sums, kv_sems.at[4]))
    for copy in kv_copies:
        copy.start()
    in_copies = []
    for stack in range(stacks):
        some = []
        for i, (own, target) in enumerate(((query, q_all), (dout, d_all))):
            column = me * (2048) + (group * 8 + first + stack * STACK) * HEAD_DIM
            some.append((own.at[:, pl.ds(pl.multiple_of(column, TILE), wide)], target, i, me))
            for shift, got in zip(SHIFTS, (got_a, got_b, got_c)):
                piece = got.at[i, :, pl.ds(stack * wide, wide)]
                some.append((piece, target, i, source_of(me, shift)))
        copies = [
            pltpu.make_async_copy(
                source,
                target.at[stack, pl.ds(aligned(place, rows), rows), :],
                in_sems.at[8 * stack + at],
            )
            for at, (source, target, i, place) in enumerate(some)
        ]
        for copy in copies:
            copy.start()
        in_copies.append(copies)

    for row in range(4):
        place = lax.broadcasted_iota(jnp.int32, (5 * TILE, TILE), 0) + row * TILE
        token = lax.broadcasted_iota(jnp.int32, (5 * TILE, TILE), 1) + block + row * TILE
        since = start[:, row * TILE : (row + 1) * TILE]
        bias[row] = jnp.where((place >= since) & (place <= token), 0.0, -1e30)
    if not has_sums:
        sums[...] = jnp.zeros_like(sums)
    for copy in kv_copies:
        copy.wait()
    for i in range(8):
        piece = keys[i * TILE : (i + 1) * TILE, :]
        keys_t[i] = piece.astype(jnp.float32).T.astype(jnp.bfloat16)

    to_exponent = math.log2(math.e) / math.sqrt(HEAD_DIM)
    scale = 1.0 / math.sqrt(HEAD_DIM)

    def step(stack, row, tiles):
        size = tiles * TILE
        tile = row + 5 - tiles
        window = pl.ds(aligned(tile, TILE), size)
        own = pl.ds(aligned(row, TILE), TILE)
        key, value = keys[window, :], values[window, :]
        q = jnp.concatenate(
            [q_all[stack, own, h * HEAD_DIM : (h + 1) * HEAD_DIM] for h in range(STACK)], axis=0
        )
        d = jnp.concatenate(
            [d_all[stack, own, h * HEAD_DIM : (h + 1) * HEAD_DIM] for h in range(STACK)], axis=0
        )
        mask = bias[row, (5 - tiles) * TILE :, :]
        scores = dot(key, q, ROWS_BY_ROWS) * to_exponent + jnp.concatenate([mask] * STACK, axis=1)
        highest = jnp.max(scores, axis=0, keepdims=True)
        weights = jnp.exp2(scores - highest)
        probs = weights * (1.0 / jnp.sum(weights, axis=0, keepdims=True))
        dprobs = dot(value, d, ROWS_BY_ROWS)
        delta = jnp.sum(probs * dprobs, axis=0, keepdims=True)
        dscores = (probs * (dprobs - delta)).astype(jnp.bfloat16)
        sums[1, window, :] += dot(probs.astype(jnp.bfloat16), d, ROWS_BY_COLUMNS)
        sums[0, window, :] += dot(dscores, q, ROWS_BY_COLUMNS)
        key_t = jnp.concatenate([keys_t[tile + i] for i in range(tiles)], axis=1)
        dq_t = dot(key_t, dscores, ROWS_BY_COLUMNS) * scale
        for h in range(STACK):
            columns = slice(h * HEAD_DIM, (h + 1) * HEAD_DIM)
            dq[stack, own, columns] = dq_t[:, columns].T.astype(jnp.bfloat16)

    def out_copy(stack, row):
        own = pl.ds(aligned(row, TILE), TILE)
        column = (group * 8 + first + stack * STACK) * HEAD_DIM
        return pltpu.make_async_copy(
            dq.at[stack, own, :],
            query_out.at[own, pl.ds(column, wide)],
            out_sems.at[stack, row],
        )

    for stack in range(stacks):
        for copy in in_copies[stack]:
            copy.wait()

        @pl.loop(0, 4)
        def _(row):
            count = scal[1 + row]
            for tiles in range(1, 6):

                @pl.when(count == tiles)
                def _():
                    step(stack, row, tiles)

            out_copy(stack, row).start()

    if ends:
        own_out[0] = sums[0, block:, :] * scale
        own_out[1] = sums[1, block:, :]
        prior_out[0] = (sums[0, :block, :] * scale).astype(jnp.bfloat16)
        prior_out[1] = sums[1, :block, :].astype(jnp.bfloat16)
    else:
        sums_out[...] = sums[...]
    for stack in range(stacks):
        for row in range(4):
            out_copy(stack, row).wait()


def attention(part, scal, start, kv_own, kv_prev, got, query, dout, query_grad, sums, ends):
    group, first, heads = part
    rows = query.shape[0]
    block = 4 * rows
    stacks = heads // STACK
    wide = STACK * HEAD_DIM
    has_query, has_sums = query_grad is not None, sums is not None
    args = [scal, start, kv_own, kv_prev, *got, query, dout]
    specs = [SMEM, VMEM] + [ANY] * 7
    aliases = {}
    if has_query:
        aliases = {len(args): 0}
        args.append(query_grad)
        specs.append(ANY)
    if has_sums:
        args.append(sums)
        specs.append(ANY)
    shapes = [jax.ShapeDtypeStruct((block, 2048), jnp.bfloat16)]
    if ends:
        shapes.append(jax.ShapeDtypeStruct((2, block, HEAD_DIM), jnp.float32))
        shapes.append(jax.ShapeDtypeStruct((2, block, HEAD_DIM), jnp.bfloat16))
    else:
        shapes.append(jax.ShapeDtypeStruct((2, 2 * block, HEAD_DIM), jnp.float32))
    return pl.pallas_call(
        functools.partial(attention_kernel, part, has_query, has_sums, ends),
        out_shape=tuple(shapes),
        in_specs=specs,
        out_specs=(ANY,) + (VMEM,) * (len(shapes) - 1),
        scratch_shapes=[
            pltpu.VMEM((stacks, block, wide), jnp.bfloat16),
            pltpu.VMEM((stacks, block, wide), jnp.bfloat16),
            pltpu.VMEM((2 * block, HEAD_DIM), jnp.bfloat16),
            pltpu.VMEM((2 * block, HEAD_DIM), jnp.bfloat16),
            pltpu.VMEM((8, HEAD_DIM, TILE), jnp.bfloat16),
            pltpu.VMEM((4, 5 * TILE, TILE), jnp.float32),
            pltpu.VMEM((2, 2 * block, HEAD_DIM), jnp.float32),
            pltpu.VMEM((stacks, block, wide), jnp.bfloat16),
            pltpu.SemaphoreType.DMA((5,)),
            pltpu.SemaphoreType.DMA((8 * stacks,)),
            pltpu.SemaphoreType.DMA((stacks, 4)),
        ],
        input_output_aliases=aliases,
        compiler_params=pltpu.CompilerParams(vmem_limit_bytes=40 * 2**20),
        cost_estimate=pl.CostEstimate(
            flops=heads * 10 * 5 * 2 * 128**3,
            bytes_accessed=heads * block * HEAD_DIM * 2 * 3,
            transcendentals=heads * 10 * 128**2,
        ),
    )(*args)


def from_behind(shard, axis, by):
    length = lax.axis_size(axis)
    pairs = [(i, i + by) for i in range(length) if 0 <= i + by < length]
    return lax.ppermute(shard, axis, pairs)


def around(pieces):
    return [
        lax.ppermute(piece, "hd", [(i, (i + shift) % 4) for i in range(4)])
        for shift, piece in zip(SHIFTS, pieces)
    ]


def per_device(query, key, value, dout, doc_ids, tile_plan):
    rows = query.shape[0]
    length = 4 * rows
    index = lax.axis_index("cp")
    me = lax.axis_index("hd").reshape(1)

    got_kv = around(cut(me, key, value, 256, 0, 256))
    got = [
        around(cut(me, query, dout, 2048, (group * 8 + first) * HEAD_DIM, heads * HEAD_DIM))
        for group, first, heads in PARTS
    ]
    kv_own = join(me, got_kv, key, value)
    kv_prev = from_behind(kv_own, "cp", 1)

    own_docs = lax.dynamic_slice_in_dim(doc_ids, index * length, length, 0)
    prior_docs = lax.dynamic_slice_in_dim(
        doc_ids, jnp.maximum(index - 1, 0) * length, length, 0
    )
    plan = lax.dynamic_index_in_dim(tile_plan, index, 0, keepdims=False)
    docs = jnp.concatenate([jnp.where(index > 0, prior_docs, -1), own_docs])
    start = jnp.sum((docs[None, :] < own_docs[:, None]).astype(jnp.int32), axis=1)
    start = jnp.where(plan != 0, start, jnp.maximum(start, length))
    counts = 5 + jnp.arange(4, dtype=jnp.int32) - start[::TILE] // TILE
    scal = jnp.concatenate([me, counts])
    start = start.reshape(1, length)

    query_grad, sums = None, None
    own, prior = [], []
    for at, part in enumerate(PARTS):
        ends = at + 1 == len(PARTS) or PARTS[at + 1][0] != part[0]
        query_grad, *more = attention(
            part, scal, start, kv_own, kv_prev, got[at], query, dout, query_grad, sums, ends
        )
        if ends:
            own.append(more[0])
            prior.append(from_behind(more[1], "cp", -1))
            sums = None
        else:
            sums = more[0]
    totals = [
        jnp.concatenate(
            [(own[g][i] + prior[g][i].astype(jnp.float32)) for g in range(2)], axis=1
        ).astype(jnp.bfloat16)
        for i in range(2)
    ]
    return query_grad, totals[0], totals[1]


def solution(mesh):
    return jax.shard_map(
        per_device,
        mesh=mesh,
        in_specs=(
            P(("cp", "hd"), None),
            P(("cp", "hd"), None),
            P(("cp", "hd"), None),
            P(("cp", "hd"), None),
            P(),
            P(),
        ),
        out_specs=(P("cp", "hd"), P("cp", "hd"), P("cp", "hd")),
        check_vma=False,
    )
```

profile of v0, /device:TPU:16, one launch (start us, length us, event | category | flops | bytes accessed | tf_op | source)
XLA Modules:
  0.0 92.7 jit_solution(3483062459115475236)
XLA Ops:
  0.6 1.7 %shard_map.85 = (bf16[2,128,256]{2,1,0:T(8,128)(2,1)}, bf16[2,128,256]{2,1,0:T(8,128)(2,1)}, bf16[2,128,256]{2,1,0:T(8,128)(2,1)}) custom-call(s32[1]{0:T(128)} %bitcast.me_ref, bf16[128,1024]{1,0:T(8,128)(2,1)} %left.6, bf16[128,1024]{1,0:T(8,128)(2,1)} %right.6), custom_call_target="tpu_custom_call" | custom-call | bytes 786432 | tf_op jit(solution)/shard_map/pallas_call | solution.py:70
  2.4 1.6 %collective-permute-start = (bf16[2,128,256]{2,1,0:T(8,128)(2,1)}, bf16[2,128,256]{2,1,0:T(8,128)(2,1)S(1)}, u32[]{:S(2)}, u32[]{:S(2)}) collective-permute-start(bf16[2,128,256]{2,1,0:T(8,128)(2,1)} %get-tuple-element.23), channel_id=1, source_target_pairs={{0,1},{1,2},{2,3},{3,0},{4,5},{5,6},{6,7},{7,4},{8,9},{9,10},{10,1... | collective-permute-start | bytes 393224 | tf_op jit(solution)/shard_map/ppermute | solution.py:308
  3.9 1.7 %collective-permute-start.1 = (bf16[2,128,256]{2,1,0:T(8,128)(2,1)}, bf16[2,128,256]{2,1,0:T(8,128)(2,1)S(1)}, u32[]{:S(2)}, u32[]{:S(2)}) collective-permute-start(bf16[2,128,256]{2,1,0:T(8,128)(2,1)} %get-tuple-element.24), channel_id=1, source_target_pairs={{0,3},{1,0},{2,1},{3,2},{4,7},{5,4},{6,5},{7,6},{8,11},{9,8},{10,9... | collective-permute-start | bytes 393224 | tf_op jit(solution)/shard_map/ppermute | solution.py:308
  5.7 1.8 %collective-permute-start.2 = (bf16[2,128,256]{2,1,0:T(8,128)(2,1)}, bf16[2,128,256]{2,1,0:T(8,128)(2,1)S(1)}, u32[]{:S(2)}, u32[]{:S(2)}) collective-permute-start(bf16[2,128,256]{2,1,0:T(8,128)(2,1)} %get-tuple-element.25), channel_id=1, source_target_pairs={{0,2},{1,3},{2,0},{3,1},{4,6},{5,7},{6,4},{7,5},{8,10},{9,11},{10,... | collective-permute-start | bytes 393224 | tf_op jit(solution)/shard_map/ppermute | solution.py:308
  7.5 2.2 %shard_map.89 = (bf16[2,128,1024]{2,1,0:T(8,128)(2,1)}, bf16[2,128,1024]{2,1,0:T(8,128)(2,1)}, bf16[2,128,1024]{2,1,0:T(8,128)(2,1)}) custom-call(s32[1]{0:T(128)} %bitcast.me_ref, bf16[128,8192]{1,0:T(8,128)(2,1)} %refs_7_.5, bf16[128,8192]{1,0:T(8,128)(2,1)} %refs_8_.5), custom_call_target="tpu_custom_call" | custom-call | bytes 3145728 | tf_op jit(solution)/shard_map/pallas_call | solution.py:70
  9.8 0.7 collective-permute-start.10
  10.4 2.6 %collective-permute-start.11 = (bf16[2,128,1024]{2,1,0:T(8,128)(2,1)}, bf16[2,128,1024]{2,1,0:T(8,128)(2,1)}, u32[]{:S(2)}, u32[]{:S(2)}) collective-permute-start(bf16[2,128,1024]{2,1,0:T(8,128)(2,1)} %get-tuple-element.33), channel_id=1, source_target_pairs={{0,3},{1,0},{2,1},{3,2},{4,7},{5,4},{6,5},{7,6},{8,11},{9,8},{10,9... | collective-permute-start | bytes 1572872 | tf_op jit(solution)/shard_map/ppermute | solution.py:308
  13.1 0.8 dynamic-slice_select_fusion
  13.9 0.4 convert_reduce_fusion
  14.2 0.6 dynamic_slice.10
  15.5 2.0 %shard_map.88 = (bf16[2,128,512]{2,1,0:T(8,128)(2,1)}, bf16[2,128,512]{2,1,0:T(8,128)(2,1)}, bf16[2,128,512]{2,1,0:T(8,128)(2,1)}) custom-call(s32[1]{0:T(128)} %bitcast.me_ref, bf16[128,8192]{1,0:T(8,128)(2,1)} %refs_7_.5, bf16[128,8192]{1,0:T(8,128)(2,1)} %refs_8_.5), custom_call_target="tpu_custom_call" | custom-call | bytes 1572864 | tf_op jit(solution)/shard_map/pallas_call | solution.py:70
  17.5 0.1 slice.27
  17.6 0.0 collective-permute-done.got_a
  17.6 0.6 collective-permute-start.12
  18.2 0.0 collective-permute-done.1.got_b
  18.2 0.4 collective-permute-start.7
  18.5 0.0 collective-permute-done.2.got_c
  18.5 0.3 copy-done.6
  18.8 0.7 copy-done.7
  19.5 1.8 %shard_map.86.refs_2_ = bf16[2,512,256]{2,1,0:T(8,128)(2,1)} custom-call(s32[1]{0:T(128)} %bitcast.me_ref, bf16[2,128,256]{2,1,0:T(8,128)(2,1)} %copy-done.5, bf16[2,128,256]{2,1,0:T(8,128)(2,1)} %copy-done.6, bf16[2,128,256]{2,1,0:T(8,128)(2,1)} %copy-done.7, bf16[128,1024]{1,0:T(8,128)(2,1)} %left.6, bf16[128,1024]{1,0:T(8,128)(2,1)} %right.6), custom_call_target="tpu_custom_call" | custom-call | bytes 1048576 | tf_op jit(solution)/shard_map/pallas_call | solution.py:100
  21.3 1.9 %collective-permute-start.3 = (bf16[2,512,256]{2,1,0:T(8,128)(2,1)}, bf16[2,512,256]{2,1,0:T(8,128)(2,1)S(1)}, u32[]{:S(2)}, u32[]{:S(2)}) collective-permute-start(bf16[2,512,256]{2,1,0:T(8,128)(2,1)} %shard_map.86.refs_2_), channel_id=1, source_target_pairs={{0,4},{4,8},{8,12},{12,16},{16,20},{20,24},{24,28},{28,32},{32,36}... | collective-permute-start | bytes 1572872 | tf_op jit(solution)/shard_map/ppermute | solution.py:303
  23.3 18.0 %collective-permute-done.7.refs_4_ = bf16[2,128,512]{2,1,0:T(8,128)(2,1)S(1)} collective-permute-done((bf16[2,128,512]{2,1,0:T(8,128)(2,1)}, bf16[2,128,512]{2,1,0:T(8,128)(2,1)S(1)}, u32[]{:S(2)}, u32[]{:S(2)}) %collective-permute-start.7) | collective-permute-done | bytes 262176 | tf_op jit(solution)/shard_map/ppermute | solution.py:308
  41.3 0.3 collective-permute-start.8
  41.6 0.0 collective-permute-done.10.refs_4_
  41.6 0.8 copy-done.3
  42.4 1.3 %collective-permute-start.9 = (bf16[2,128,512]{2,1,0:T(8,128)(2,1)}, bf16[2,128,512]{2,1,0:T(8,128)(2,1)}, u32[]{:S(2)}, u32[]{:S(2)}) collective-permute-start(bf16[2,128,512]{2,1,0:T(8,128)(2,1)} %get-tuple-element.31), channel_id=1, source_target_pairs={{0,2},{1,3},{2,0},{3,1},{4,6},{5,7},{6,4},{7,5},{8,10},{9,11},{10,... | collective-permute-start | bytes 786440 | tf_op jit(solution)/shard_map/ppermute | solution.py:308
  43.7 0.1 pad_add_fusion.1.refs_0_
  43.8 2.1 %shard_map.87 = (bf16[2,128,512]{2,1,0:T(8,128)(2,1)}, bf16[2,128,512]{2,1,0:T(8,128)(2,1)}, bf16[2,128,512]{2,1,0:T(8,128)(2,1)}) custom-call(s32[1]{0:T(128)} %bitcast.me_ref, bf16[128,8192]{1,0:T(8,128)(2,1)} %refs_7_.5, bf16[128,8192]{1,0:T(8,128)(2,1)} %refs_8_.5), custom_call_target="tpu_custom_call" | custom-call | bytes 1572864 | tf_op jit(solution)/shard_map/pallas_call | solution.py:70
  45.9 0.0 collective-permute-done.11.refs_5_
  45.9 0.9 collective-permute-start.4
  46.8 0.0 collective-permute-done.12.refs_6_
  46.8 2.4 %collective-permute-start.5 = (bf16[2,128,512]{2,1,0:T(8,128)(2,1)}, bf16[2,128,512]{2,1,0:T(8,128)(2,1)S(1)}, u32[]{:S(2)}, u32[]{:S(2)}) collective-permute-start(bf16[2,128,512]{2,1,0:T(8,128)(2,1)} %get-tuple-element.27), channel_id=1, source_target_pairs={{0,3},{1,0},{2,1},{3,2},{4,7},{5,4},{6,5},{7,6},{8,11},{9,8},{10,9... | collective-permute-start | bytes 786440 | tf_op jit(solution)/shard_map/ppermute | solution.py:308
  49.2 0.0 collective-permute-done.3.refs_3_
  49.2 1.6 %collective-permute-start.6 = (bf16[2,128,512]{2,1,0:T(8,128)(2,1)}, bf16[2,128,512]{2,1,0:T(8,128)(2,1)S(1)}, u32[]{:S(2)}, u32[]{:S(2)}) collective-permute-start(bf16[2,128,512]{2,1,0:T(8,128)(2,1)} %get-tuple-element.28), channel_id=1, source_target_pairs={{0,2},{1,3},{2,0},{3,1},{4,6},{5,7},{6,4},{7,5},{8,10},{9,11},{10,... | collective-permute-start | bytes 786440 | tf_op jit(solution)/shard_map/ppermute | solution.py:308
  50.8 1.6 %copy-done.1 = bf16[128,8192]{1,0:T(8,128)(2,1)S(1)} copy-done((bf16[128,8192]{1,0:T(8,128)(2,1)S(1)}, bf16[128,8192]{1,0:T(8,128)(2,1)}, u32[]{:S(2)}) %copy-start.1) | copy-done | bytes 2097176
  52.4 1.0 %copy-done.4 = bf16[2,128,1024]{2,1,0:T(8,128)(2,1)S(1)} copy-done((bf16[2,128,1024]{2,1,0:T(8,128)(2,1)S(1)}, bf16[2,128,1024]{2,1,0:T(8,128)(2,1)}, u32[]{:S(2)}) %copy-start.4) | copy-done | bytes 524312
  53.5 10.9 %shard_map.90 = (bf16[512,2048]{1,0:T(8,128)(2,1)}, f32[2,512,128]{2,1,0:T(8,128)S(1)}, bf16[2,512,128]{2,1,0:T(8,128)(2,1)S(1)}) custom-call(s32[5]{0:T(128)S(1)} %pad_add_fusion.1.refs_0_, s32[1,512]{1,0:T(1,128)S(1)} %broadcast_select_fusion.refs_1_, bf16[2,512,256]{2,1,0:T(8,128)(2,1)S(1)} %copy-done.2, ...), custom_call_target="tpu_custom_call" | custom-call | flops 1677721600 | bytes 3145728 | tf_op jit(solution)/shard_map/pallas_call | solution.py:272
  64.4 0.0 collective-permute-done.8.refs_5_
  64.4 4.3 %collective-permute-start.13 = (bf16[2,512,128]{2,1,0:T(8,128)(2,1)S(1)}, bf16[2,512,128]{2,1,0:T(8,128)(2,1)S(1)}, u32[]{:S(2)}, u32[]{:S(2)}) collective-permute-start(bf16[2,512,128]{2,1,0:T(8,128)(2,1)S(1)} %get-tuple-element.40), channel_id=1, source_target_pairs={{4,0},{8,4},{12,8},{16,12},{20,16},{24,20},{28,24},{32,28},{36,32}... | collective-permute-start | bytes 786440 | tf_op jit(solution)/shard_map/ppermute | solution.py:303
  68.7 0.0 collective-permute-done.9.refs_6_
  68.8 6.9 %shard_map.91 = (bf16[512,2048]{1,0:T(8,128)(2,1)}, f32[2,1024,128]{2,1,0:T(8,128)S(1)}) custom-call(s32[5]{0:T(128)S(1)} %pad_add_fusion.1.refs_0_, s32[1,512]{1,0:T(1,128)S(1)} %broadcast_select_fusion.refs_1_, bf16[2,512,256]{2,1,0:T(8,128)(2,1)S(1)} %copy-done.2, ...), custom_call_target="tpu_custom_call", output_to_operand_aliasing={{0}: (9, {})} | custom-call | flops 838860800 | bytes 1572864 | tf_op jit(solution)/shard_map/pallas_call | solution.py:272
  75.7 0.0 collective-permute-done.5.refs_5_
  75.7 7.0 %shard_map.92 = (bf16[512,2048]{1,0:T(8,128)(2,1)}, f32[2,512,128]{2,1,0:T(8,128)S(1)}, bf16[2,512,128]{2,1,0:T(8,128)(2,1)S(1)}) custom-call(s32[5]{0:T(128)S(1)} %pad_add_fusion.1.refs_0_, s32[1,512]{1,0:T(1,128)S(1)} %broadcast_select_fusion.refs_1_, bf16[2,512,256]{2,1,0:T(8,128)(2,1)S(1)} %copy-done.2, ...), custom_call_target="tpu_custom_call", output_to_operand_aliasing={{0}: (9, {})} | custom-call | flops 838860800 | bytes 1572864 | tf_op jit(solution)/shard_map/pallas_call | solution.py:272
  82.7 5.1 %collective-permute-start.14 = (bf16[2,512,128]{2,1,0:T(8,128)(2,1)S(1)}, bf16[2,512,128]{2,1,0:T(8,128)(2,1)S(1)}, u32[]{:S(2)}, u32[]{:S(2)}) collective-permute-start(bf16[2,512,128]{2,1,0:T(8,128)(2,1)S(1)} %get-tuple-element.42), channel_id=1, source_target_pairs={{4,0},{8,4},{12,8},{16,12},{20,16},{24,20},{28,24},{32,28},{36,32}... | collective-permute-start | bytes 786440 | tf_op jit(solution)/shard_map/ppermute | solution.py:303
  87.9 0.1 fusion.2
  87.9 3.8 %collective-permute-done.14 = bf16[2,512,128]{2,1,0:T(8,128)(2,1)S(1)} collective-permute-done((bf16[2,512,128]{2,1,0:T(8,128)(2,1)S(1)}, bf16[2,512,128]{2,1,0:T(8,128)(2,1)S(1)}, u32[]{:S(2)}, u32[]{:S(2)}) %collective-permute-start.14) | collective-permute-done | bytes 262176 | tf_op jit(solution)/shard_map/ppermute | solution.py:303
  91.7 0.1 fusion.3
  91.8 0.9 pad_maximum_fusion
  (20 shorter events, 0.1 us)
Async XLA Ops:
  2.4 15.2 %collective-permute-start = (bf16[2,128,256]{2,1,0:T(8,128)(2,1)}, bf16[2,128,256]{2,1,0:T(8,128)(2,1)S(1)}, u32[]{:S(2)}, u32[]{:S(2)}) collective-permute-start(bf16[2,128,256]{2,1,0:T(8,128)(2,1)} %get-tuple-element.23), channel_id=1, source_target_pairs={{0,1},{1,2},{2,3},{3,0},{4,5},{5,6},{6,7},{7,4},{8,9},{9,10},{10,1... | collective-permute-start | bytes 393224 | tf_op jit(solution)/shard_map/ppermute | solution.py:308
  3.9 14.2 %collective-permute-start.1 = (bf16[2,128,256]{2,1,0:T(8,128)(2,1)}, bf16[2,128,256]{2,1,0:T(8,128)(2,1)S(1)}, u32[]{:S(2)}, u32[]{:S(2)}) collective-permute-start(bf16[2,128,256]{2,1,0:T(8,128)(2,1)} %get-tuple-element.24), channel_id=1, source_target_pairs={{0,3},{1,0},{2,1},{3,2},{4,7},{5,4},{6,5},{7,6},{8,11},{9,8},{10,9... | collective-permute-start | bytes 393224 | tf_op jit(solution)/shard_map/ppermute | solution.py:308
  5.7 8.5 %copy-start.8 = (s32[64]{0:T(128)S(1)}, s32[64]{0:T(128)}, u32[]{:S(2)}) copy-start(s32[64]{0:T(128)} %param.11) | copy-start | bytes 772
  5.7 12.8 %collective-permute-start.2 = (bf16[2,128,256]{2,1,0:T(8,128)(2,1)}, bf16[2,128,256]{2,1,0:T(8,128)(2,1)S(1)}, u32[]{:S(2)}, u32[]{:S(2)}) collective-permute-start(bf16[2,128,256]{2,1,0:T(8,128)(2,1)} %get-tuple-element.25), channel_id=1, source_target_pairs={{0,2},{1,3},{2,0},{3,1},{4,6},{5,7},{6,4},{7,5},{8,10},{9,11},{10,... | collective-permute-start | bytes 393224 | tf_op jit(solution)/shard_map/ppermute | solution.py:308
  9.8 31.8 %collective-permute-start.10 = (bf16[2,128,1024]{2,1,0:T(8,128)(2,1)}, bf16[2,128,1024]{2,1,0:T(8,128)(2,1)S(1)}, u32[]{:S(2)}, u32[]{:S(2)}) collective-permute-start(bf16[2,128,1024]{2,1,0:T(8,128)(2,1)} %get-tuple-element.32), channel_id=1, source_target_pairs={{0,1},{1,2},{2,3},{3,0},{4,5},{5,6},{6,7},{7,4},{8,9},{9,10},{10,1... | collective-permute-start | bytes 1572872 | tf_op jit(solution)/shard_map/ppermute | solution.py:308
  10.4 35.5 %collective-permute-start.11 = (bf16[2,128,1024]{2,1,0:T(8,128)(2,1)}, bf16[2,128,1024]{2,1,0:T(8,128)(2,1)}, u32[]{:S(2)}, u32[]{:S(2)}) collective-permute-start(bf16[2,128,1024]{2,1,0:T(8,128)(2,1)} %get-tuple-element.33), channel_id=1, source_target_pairs={{0,3},{1,0},{2,1},{3,2},{4,7},{5,4},{6,5},{7,6},{8,11},{9,8},{10,9... | collective-permute-start | bytes 1572872 | tf_op jit(solution)/shard_map/ppermute | solution.py:308
  17.6 1.0 %copy-start.5 = (bf16[2,128,256]{2,1,0:T(8,128)(2,1)}, bf16[2,128,256]{2,1,0:T(8,128)(2,1)S(1)}, u32[]{:S(2)}) copy-start(bf16[2,128,256]{2,1,0:T(8,128)(2,1)S(1)} %collective-permute-done.got_a) | copy-start | bytes 393220
  17.6 29.2 %collective-permute-start.12 = (bf16[2,128,1024]{2,1,0:T(8,128)(2,1)}, bf16[2,128,1024]{2,1,0:T(8,128)(2,1)}, u32[]{:S(2)}, u32[]{:S(2)}) collective-permute-start(bf16[2,128,1024]{2,1,0:T(8,128)(2,1)} %get-tuple-element.34), channel_id=1, source_target_pairs={{0,2},{1,3},{2,0},{3,1},{4,6},{5,7},{6,4},{7,5},{8,10},{9,11},{10,... | collective-permute-start | bytes 1572872 | tf_op jit(solution)/shard_map/ppermute | solution.py:308
  18.2 0.6 copy-start.6
  18.2 23.1 %collective-permute-start.7 = (bf16[2,128,512]{2,1,0:T(8,128)(2,1)}, bf16[2,128,512]{2,1,0:T(8,128)(2,1)S(1)}, u32[]{:S(2)}, u32[]{:S(2)}) collective-permute-start(bf16[2,128,512]{2,1,0:T(8,128)(2,1)} %get-tuple-element.29), channel_id=1, source_target_pairs={{0,1},{1,2},{2,3},{3,0},{4,5},{5,6},{6,7},{7,4},{8,9},{9,10},{10,1... | collective-permute-start | bytes 786440 | tf_op jit(solution)/shard_map/ppermute | solution.py:308
  18.8 0.7 copy-start.7
  21.3 27.9 %collective-permute-start.3 = (bf16[2,512,256]{2,1,0:T(8,128)(2,1)}, bf16[2,512,256]{2,1,0:T(8,128)(2,1)S(1)}, u32[]{:S(2)}, u32[]{:S(2)}) collective-permute-start(bf16[2,512,256]{2,1,0:T(8,128)(2,1)} %shard_map.86.refs_2_), channel_id=1, source_target_pairs={{0,4},{4,8},{8,12},{12,16},{16,20},{20,24},{24,28},{28,32},{32,36}... | collective-permute-start | bytes 1572872 | tf_op jit(solution)/shard_map/ppermute | solution.py:303
  41.3 23.1 %collective-permute-start.8 = (bf16[2,128,512]{2,1,0:T(8,128)(2,1)}, bf16[2,128,512]{2,1,0:T(8,128)(2,1)}, u32[]{:S(2)}, u32[]{:S(2)}) collective-permute-start(bf16[2,128,512]{2,1,0:T(8,128)(2,1)} %get-tuple-element.30), channel_id=1, source_target_pairs={{0,3},{1,0},{2,1},{3,2},{4,7},{5,4},{6,5},{7,6},{8,11},{9,8},{10,9... | collective-permute-start | bytes 786440 | tf_op jit(solution)/shard_map/ppermute | solution.py:308
  41.6 0.8 copy-start.3
  42.4 26.3 %collective-permute-start.9 = (bf16[2,128,512]{2,1,0:T(8,128)(2,1)}, bf16[2,128,512]{2,1,0:T(8,128)(2,1)}, u32[]{:S(2)}, u32[]{:S(2)}) collective-permute-start(bf16[2,128,512]{2,1,0:T(8,128)(2,1)} %get-tuple-element.31), channel_id=1, source_target_pairs={{0,2},{1,3},{2,0},{3,1},{4,6},{5,7},{6,4},{7,5},{8,10},{9,11},{10,... | collective-permute-start | bytes 786440 | tf_op jit(solution)/shard_map/ppermute | solution.py:308
  43.8 7.1 %copy-start = (bf16[128,8192]{1,0:T(8,128)(2,1)S(1)}, bf16[128,8192]{1,0:T(8,128)(2,1)}, u32[]{:S(2)}) copy-start(bf16[128,8192]{1,0:T(8,128)(2,1)} %refs_7_.5) | copy-start | bytes 6291460
  43.8 7.1 %copy-start.2 = (bf16[2,512,256]{2,1,0:T(8,128)(2,1)S(1)}, bf16[2,512,256]{2,1,0:T(8,128)(2,1)}, u32[]{:S(2)}) copy-start(bf16[2,512,256]{2,1,0:T(8,128)(2,1)} %shard_map.86.refs_2_) | copy-start | bytes 1572868
  45.9 29.8 %collective-permute-start.4 = (bf16[2,128,512]{2,1,0:T(8,128)(2,1)}, bf16[2,128,512]{2,1,0:T(8,128)(2,1)S(1)}, u32[]{:S(2)}, u32[]{:S(2)}) collective-permute-start(bf16[2,128,512]{2,1,0:T(8,128)(2,1)} %get-tuple-element.26), channel_id=1, source_target_pairs={{0,1},{1,2},{2,3},{3,0},{4,5},{5,6},{6,7},{7,4},{8,9},{9,10},{10,1... | collective-permute-start | bytes 786440 | tf_op jit(solution)/shard_map/ppermute | solution.py:308
  46.8 28.9 %collective-permute-start.5 = (bf16[2,128,512]{2,1,0:T(8,128)(2,1)}, bf16[2,128,512]{2,1,0:T(8,128)(2,1)S(1)}, u32[]{:S(2)}, u32[]{:S(2)}) collective-permute-start(bf16[2,128,512]{2,1,0:T(8,128)(2,1)} %get-tuple-element.27), channel_id=1, source_target_pairs={{0,3},{1,0},{2,1},{3,2},{4,7},{5,4},{6,5},{7,6},{8,11},{9,8},{10,9... | collective-permute-start | bytes 786440 | tf_op jit(solution)/shard_map/ppermute | solution.py:308
  49.2 26.5 %collective-permute-start.6 = (bf16[2,128,512]{2,1,0:T(8,128)(2,1)}, bf16[2,128,512]{2,1,0:T(8,128)(2,1)S(1)}, u32[]{:S(2)}, u32[]{:S(2)}) collective-permute-start(bf16[2,128,512]{2,1,0:T(8,128)(2,1)} %get-tuple-element.28), channel_id=1, source_target_pairs={{0,2},{1,3},{2,0},{3,1},{4,6},{5,7},{6,4},{7,5},{8,10},{9,11},{10,... | collective-permute-start | bytes 786440 | tf_op jit(solution)/shard_map/ppermute | solution.py:308
  50.8 1.6 %copy-start.1 = (bf16[128,8192]{1,0:T(8,128)(2,1)S(1)}, bf16[128,8192]{1,0:T(8,128)(2,1)}, u32[]{:S(2)}) copy-start(bf16[128,8192]{1,0:T(8,128)(2,1)} %refs_8_.5) | copy-start | bytes 6291460
  52.4 1.0 %copy-start.4 = (bf16[2,128,1024]{2,1,0:T(8,128)(2,1)S(1)}, bf16[2,128,1024]{2,1,0:T(8,128)(2,1)}, u32[]{:S(2)}) copy-start(bf16[2,128,1024]{2,1,0:T(8,128)(2,1)} %copy-done.3) | copy-start | bytes 1572868
  64.4 23.4 %collective-permute-start.13 = (bf16[2,512,128]{2,1,0:T(8,128)(2,1)S(1)}, bf16[2,512,128]{2,1,0:T(8,128)(2,1)S(1)}, u32[]{:S(2)}, u32[]{:S(2)}) collective-permute-start(bf16[2,512,128]{2,1,0:T(8,128)(2,1)S(1)} %get-tuple-element.40), channel_id=1, source_target_pairs={{4,0},{8,4},{12,8},{16,12},{20,16},{24,20},{28,24},{32,28},{36,32}... | collective-permute-start | bytes 786440 | tf_op jit(solution)/shard_map/ppermute | solution.py:303
  82.7 9.0 %collective-permute-start.14 = (bf16[2,512,128]{2,1,0:T(8,128)(2,1)S(1)}, bf16[2,512,128]{2,1,0:T(8,128)(2,1)S(1)}, u32[]{:S(2)}, u32[]{:S(2)}) collective-permute-start(bf16[2,512,128]{2,1,0:T(8,128)(2,1)S(1)} %get-tuple-element.42), channel_id=1, source_target_pairs={{4,0},{8,4},{12,8},{16,12},{20,16},{24,20},{28,24},{32,28},{36,32}... | collective-permute-start | bytes 786440 | tf_op jit(solution)/shard_map/ppermute | solution.py:303
where the time goes:
time: 93.1 us; the launch traced here: 92.7 us
  Pallas kernels  34.8 us (37%)
  starting transfers between devices  27.2 us (29%)
  waiting for transfers between devices  21.9 us (24%)
  local copies, waits for them, and re-layouts  5.08 us (5%)
  other arithmetic  2.22 us (2%)
  between operations  1.49 us (2%)
    pallas_call x3, Pallas kernels, attention(): pl.pallas_call(functools.partial(attention_kernel, part, has_query, has_s...  24.9 us
    ppermute x12, waiting for transfers between devices, around(): lax.ppermute(piece, 'hd', [(i, (i + shift) % 4) for i in range(4)])  18.1 us
    ppermute x12, starting transfers between devices, around(): lax.ppermute(piece, 'hd', [(i, (i + shift) % 4) for i in range(4)])  15.9 us
    ppermute x3, starting transfers between devices, from_behind(): return lax.ppermute(shard, axis, pairs)  11.4 us
    pallas_call x4, Pallas kernels, cut(): pl.pallas_call(functools.partial(cut_kernel, (share, first, width)), out_...  8.07 us
    unnamed x18, local copies, waits for them, and re-layouts  4.39 us
    ppermute x3, waiting for transfers between devices, from_behind(): return lax.ppermute(shard, axis, pairs)  3.79 us
  transfers between devices with their start and end apart: 15, of which 2 were waited for; matrix products, arithmetic and copies ran while one was open for 2% of the time, Pallas kernels for 36%

commit v1 on v0

v1 whole, which is shorter than its diff:
```python
import functools
import math

import jax
import jax.numpy as jnp
from jax import lax
from jax.experimental import pallas as pl
from jax.experimental.pallas import tpu as pltpu
from jax.sharding import PartitionSpec as P

HEAD_DIM = 128
TILE = 128
STACK = 4
SHIFTS = (1, -1, 2)
SENT = ((0, 8), (8, 4), (12, 4))
PARTS = ((0, 0, 8, 0), (1, 0, 4, 1), (1, 4, 4, 2))

ANY = pl.BlockSpec(memory_space=pl.ANY)
HBM = pl.BlockSpec(memory_space=pltpu.HBM)
VMEM = pl.BlockSpec(memory_space=pltpu.VMEM)
SMEM = pl.BlockSpec(memory_space=pltpu.SMEM)
ROWS_BY_ROWS = (((1,), (1,)), ((), ()))
ROWS_BY_COLUMNS = (((1,), (0,)), ((), ()))


def dot(left, right, dims):
    return lax.dot_general(left, right, dims, preferred_element_type=jnp.float32)


def aligned(index, unit):
    return pl.multiple_of(index * unit, unit)


def source_of(me, shift):
    return lax.rem(me - shift + 4, 4)


def cut_kernel(share, first, width, shifts, me_ref, left, right, *refs):
    for shift, out in zip(shifts, refs[-len(shifts) :]):
        to = lax.rem(me_ref[0] + shift + 4, 4)
        columns = pl.ds(pl.multiple_of(to * share + first, TILE), width)
        out[0] = left[:, columns]
        out[1] = right[:, columns]


def cut(name, me, left, right, share, first, width, shifts, after=()):
    rows, count = left.shape[0], len(shifts)
    shape = jax.ShapeDtypeStruct((2, rows, width), left.dtype)
    return pl.pallas_call(
        functools.partial(cut_kernel, share, first, width, shifts),
        out_shape=(shape,) * count,
        in_specs=[SMEM, VMEM, VMEM] + [ANY] * len(after),
        out_specs=(VMEM,) * count,
        cost_estimate=pl.CostEstimate(
            flops=0, bytes_accessed=4 * count * rows * width * 2, transcendentals=0
        ),
        compiler_params=pltpu.CompilerParams(vmem_limit_bytes=16 * 2**20),
        name=name,
    )(me, left, right, *after)


def open_kernel(me_ref, key, value, query, dout, *refs):
    *outs, sems = refs
    me = me_ref[0]
    copies = []
    for out, shift, pair in zip(
        outs,
        (*SHIFTS, *SHIFTS[:2], 0),
        ((key, value),) * 3 + ((query, dout),) * 3,
    ):
        to = lax.rem(me + shift + 4, 4)
        for i, array in enumerate(pair):
            columns = pl.ds(aligned(to, array.shape[1] // 4), out.shape[2])
            copies.append(
                pltpu.make_async_copy(array.at[:, columns], out.at[i], sems.at[len(copies)])
            )
    for copy in copies:
        copy.start()
    for copy in copies:
        copy.wait()


def open_cut(me, key, value, query, dout):
    rows = key.shape[0]
    shapes = [jax.ShapeDtypeStruct((2, rows, 256), key.dtype)] * 3
    shapes += [jax.ShapeDtypeStruct((2, rows, SENT[0][1] * HEAD_DIM), key.dtype)] * 3
    return pl.pallas_call(
        open_kernel,
        out_shape=tuple(shapes),
        in_specs=[SMEM] + [ANY] * 4,
        out_specs=(VMEM,) * 6,
        scratch_shapes=[pltpu.SemaphoreType.DMA((12,))],
        cost_estimate=pl.CostEstimate(flops=0, bytes_accessed=4 * 2**20, transcendentals=0),
        name="open_cut",
    )(me, key, value, query, dout)


def join_kernel(width, me_ref, got_a, got_b, got_c, left, right, out):
    me = me_ref[0]
    rows = left.shape[0]
    columns = pl.ds(aligned(me, width), width)
    for i, array in enumerate((left, right)):
        out[i, pl.ds(aligned(me, rows), rows), :] = array[:, columns]
    for shift, got in zip(SHIFTS, (got_a, got_b, got_c)):
        out[:, pl.ds(aligned(source_of(me, shift), rows), rows), :] = got[...]


def join(me, got, left, right):
    rows, width = got[0].shape[1:]
    return pl.pallas_call(
        functools.partial(join_kernel, width),
        out_shape=jax.ShapeDtypeStruct((2, 4 * rows, width), left.dtype),
        in_specs=[SMEM] + [VMEM] * 5,
        out_specs=VMEM,
        cost_estimate=pl.CostEstimate(
            flops=0, bytes_accessed=16 * rows * width * 2, transcendentals=0
        ),
        compiler_params=pltpu.CompilerParams(vmem_limit_bytes=16 * 2**20),
        name="join",
    )(me, *got, left, right)


def prepare_kernel(start, kv_own, kv_prev, kv, keys_t, bias):
    block = kv_own.shape[1]
    kv[:, :block, :] = kv_prev[...]
    kv[:, block:, :] = kv_own[...]
    for row in range(4):
        place = lax.broadcasted_iota(jnp.int32, (5 * TILE, TILE), 0) + row * TILE
        token = lax.broadcasted_iota(jnp.int32, (5 * TILE, TILE), 1) + block + row * TILE
        since = start[:, row * TILE : (row + 1) * TILE]
        bias[row] = jnp.where((place >= since) & (place <= token), 0.0, -1e30)
    for j, source in enumerate((kv_prev, kv_own)):
        for group in range(2):
            for i in range(4):
                piece = source[
                    0, i * TILE : (i + 1) * TILE, group * HEAD_DIM : (group + 1) * HEAD_DIM
                ]
                keys_t[group, 4 * j + i] = piece.T


def prepare(start, kv_own, kv_prev):
    block, width = kv_own.shape[1:]
    return pl.pallas_call(
        prepare_kernel,
        out_shape=(
            jax.ShapeDtypeStruct((2, 2 * block, width), jnp.bfloat16),
            jax.ShapeDtypeStruct((2, 8, HEAD_DIM, TILE), jnp.bfloat16),
            jax.ShapeDtypeStruct((4, 5 * TILE, TILE), jnp.float32),
        ),
        in_specs=[VMEM] * 3,
        out_specs=(VMEM,) * 3,
        cost_estimate=pl.CostEstimate(
            flops=0, bytes_accessed=8 * block * width * 2, transcendentals=0
        ),
        compiler_params=pltpu.CompilerParams(vmem_limit_bytes=16 * 2**20),
        name="prepare",
    )(start, kv_own, kv_prev)


def attention_kernel(part, begins, ends, passes, *refs):
    group, first, heads, sent = part
    offset = group * 8 + first - SENT[sent][0]
    stacks = heads // STACK
    wide = STACK * HEAD_DIM
    refs = list(refs)
    scal, *pieces, kv, keys_t, bias = refs[:8]
    refs = refs[8 + (first + group > 0) :]
    sums_in = None if begins else refs.pop(0)
    refs = refs[passes:]
    query_out, sums = refs.pop(0), refs.pop(0)
    prior_out = refs.pop(0) if ends else None
    refs = refs[passes:]
    q_all, d_all, dq, out_sems = refs
    me = scal[0]
    block = kv.shape[1] // 2
    lanes = slice(group * HEAD_DIM, (group + 1) * HEAD_DIM)

    for shift, piece in zip((*SHIFTS, 0), pieces):
        row = source_of(me, shift)
        for stack in range(stacks):
            for h in range(STACK):
                head = offset + stack * STACK + h
                columns = slice(head * HEAD_DIM, (head + 1) * HEAD_DIM)
                at = slice(h * TILE, (h + 1) * TILE)
                q_all[stack, row, at, :] = piece[0, :, columns]
                d_all[stack, row, at, :] = piece[1, :, columns]
    if begins:
        sums[...] = jnp.zeros_like(sums)
    else:
        sums[...] = sums_in[...]

    to_exponent = math.log2(math.e) / math.sqrt(HEAD_DIM)
    scale = 1.0 / math.sqrt(HEAD_DIM)

    def step(stack, row, tiles):
        tile = row + 5 - tiles
        window = pl.ds(aligned(tile, TILE), tiles * TILE)
        key, value = kv[0, window, lanes], kv[1, window, lanes]
        q, d = q_all[stack, row], d_all[stack, row]
        mask = bias[row, (5 - tiles) * TILE :, :]
        scores = dot(key, q, ROWS_BY_ROWS) * to_exponent + jnp.concatenate([mask] * STACK, axis=1)
        highest = jnp.max(scores, axis=0, keepdims=True)
        weights = jnp.exp2(scores - highest)
        probs = weights * (1.0 / jnp.sum(weights, axis=0, keepdims=True))
        dprobs = dot(value, d, ROWS_BY_ROWS)
        delta = jnp.sum(probs * dprobs, axis=0, keepdims=True)
        dscores = (probs * (dprobs - delta)).astype(jnp.bfloat16)
        sums[1, window, :] += dot(probs.astype(jnp.bfloat16), d, ROWS_BY_COLUMNS)
        sums[0, window, :] += dot(dscores, q, ROWS_BY_COLUMNS)
        key_t = jnp.concatenate([keys_t[group, tile + i] for i in range(tiles)], axis=1)
        dq_t = dot(key_t, dscores, ROWS_BY_COLUMNS) * scale
        own = pl.ds(aligned(row, TILE), TILE)
        for h in range(STACK):
            columns = slice(h * HEAD_DIM, (h + 1) * HEAD_DIM)
            dq[stack, own, columns] = dq_t[:, columns].T.astype(jnp.bfloat16)

    def out_copy(stack, row):
        own = pl.ds(aligned(row, TILE), TILE)
        column = (group * 8 + first + stack * STACK) * HEAD_DIM
        return pltpu.make_async_copy(
            dq.at[stack, own, :],
            query_out.at[own, pl.ds(column, wide)],
            out_sems.at[stack, row],
        )

    for stack in range(stacks):

        @pl.loop(0, 4)
        def _(row):
            count = scal[1 + row]
            for tiles in range(1, 6):

                @pl.when(count == tiles)
                def _():
                    step(stack, row, tiles)

            out_copy(stack, row).start()

    if ends:
        prior_out[0] = (sums[0, :block, :] * scale).astype(jnp.bfloat16)
        prior_out[1] = sums[1, :block, :].astype(jnp.bfloat16)
    for stack in range(stacks):
        for row in range(4):
            out_copy(stack, row).wait()


def attention(name, part, scal, pieces, ready, query_grad, sums, ends, passed):
    group, first, heads, sent = part
    rows = pieces[0].shape[1]
    block = 4 * rows
    stacks = heads // STACK
    wide = STACK * HEAD_DIM
    args = [scal, *pieces, *ready]
    specs = [SMEM] + [VMEM] * 7
    shapes = [jax.ShapeDtypeStruct((block, 2048), jnp.bfloat16)]
    aliases = {}
    if query_grad is not None:
        aliases[len(args)] = 0
        args.append(query_grad)
        specs.append(ANY)
    if sums is not None:
        args.append(sums)
        specs.append(VMEM)
    shapes.append(jax.ShapeDtypeStruct((2, 2 * block, HEAD_DIM), jnp.float32))
    if ends:
        shapes.append(jax.ShapeDtypeStruct((2, block, HEAD_DIM), jnp.bfloat16))
    out_specs = [ANY] + [VMEM] * (len(shapes) - 1)
    for array in passed:
        aliases[len(args)] = len(shapes)
        args.append(array)
        specs.append(ANY)
        shapes.append(jax.ShapeDtypeStruct(array.shape, array.dtype))
        out_specs.append(ANY)
    return pl.pallas_call(
        functools.partial(attention_kernel, part, sums is None, ends, len(passed)),
        out_shape=tuple(shapes),
        in_specs=specs,
        out_specs=tuple(out_specs),
        scratch_shapes=[
            pltpu.VMEM((stacks, 4, STACK * TILE, HEAD_DIM), jnp.bfloat16),
            pltpu.VMEM((stacks, 4, STACK * TILE, HEAD_DIM), jnp.bfloat16),
            pltpu.VMEM((stacks, block, wide), jnp.bfloat16),
            pltpu.SemaphoreType.DMA((stacks, 4)),
        ],
        input_output_aliases=aliases,
        compiler_params=pltpu.CompilerParams(vmem_limit_bytes=24 * 2**20),
        cost_estimate=pl.CostEstimate(
            flops=heads * 10 * 5 * 2 * 128**3,
            bytes_accessed=heads * block * HEAD_DIM * 2 * 3,
            transcendentals=heads * 10 * 128**2,
        ),
        name=name,
    )(*args)


def from_behind(shard, axis, by):
    length = lax.axis_size(axis)
    pairs = [(i, i + by) for i in range(length) if 0 <= i + by < length]
    return lax.ppermute(shard, axis, pairs)


def around(pieces):
    return [
        lax.ppermute(piece, "hd", [(i, (i + shift) % 4) for i in range(4)])
        for shift, piece in zip(SHIFTS, pieces)
    ]


def per_device(query, key, value, dout, doc_ids, tile_plan):
    rows = query.shape[0]
    length = 4 * rows
    index = lax.axis_index("cp")
    me = lax.axis_index("hd").reshape(1)

    opened = open_cut(me, key, value, query, dout)
    got_kv = around(opened[:3])
    kv_own = join(me, got_kv, key, value)
    kv_prev = from_behind(kv_own, "cp", 1)
    own_docs = lax.dynamic_slice_in_dim(doc_ids, index * length, length, 0)
    prior_docs = lax.dynamic_slice_in_dim(
        doc_ids, jnp.maximum(index - 1, 0) * length, length, 0
    )
    plan = lax.dynamic_index_in_dim(tile_plan, index, 0, keepdims=False)
    docs = jnp.concatenate([jnp.where(index > 0, prior_docs, -1), own_docs])
    start = jnp.sum((docs[None, :] < own_docs[:, None]).astype(jnp.int32), axis=1)
    start = jnp.where(plan != 0, start, jnp.maximum(start, length))
    counts = 5 + jnp.arange(4, dtype=jnp.int32) - start[::TILE] // TILE
    scal = jnp.concatenate([me, counts])
    start = start.reshape(1, length)

    ready = prepare(start, kv_own, kv_prev)

    def cut_heads(at, shifts, after):
        first, heads = SENT[at]
        name = "cut_%d" % at
        begin, width = first * HEAD_DIM, heads * HEAD_DIM
        return cut(name, me, query, dout, 2048, begin, width, shifts, after)

    *sent, own_a = opened[3:]
    sent_a = [*sent, *cut_heads(0, (2,), got_kv[:1])]
    sent, own_b = cut_heads(1, (1, 0), (kv_own,))
    sent_b = [sent, *cut_heads(1, (-1, 2), ready)]
    got_a = around(sent_a)
    *sent_c, own_c = cut_heads(2, (1, -1, 0), got_a[2:])
    pieces = [[*got_a, own_a], [*around(sent_b), own_b]]

    query_grad, sums, passed = None, None, []
    total, prior = [], []
    for at, part in enumerate(PARTS):
        ends = at + 1 == len(PARTS) or PARTS[at + 1][0] != part[0]
        query_grad, sums, *more = attention(
            "attend_%d" % at,
            part,
            scal,
            pieces[part[3]],
            ready,
            query_grad,
            sums,
            ends,
            passed,
        )
        if at == 0:
            sent_c += cut_heads(2, (2,), more)
            pieces.append([*around(sent_c), own_c])
        if passed:
            prior.append(from_behind(more.pop(), "cp", -1))
        passed = []
        if ends:
            total.append(sums[:, length:, :])
            passed = more
            sums = None
    prior.append(from_behind(passed[0], "cp", -1))
    scale = 1.0 / math.sqrt(HEAD_DIM)
    key_grad, value_grad = [
        jnp.concatenate(
            [total[g][i] * factor + prior[g][i].astype(jnp.float32) for g in range(2)], axis=1
        ).astype(jnp.bfloat16)
        for i, factor in enumerate((scale, 1.0))
    ]
    return query_grad, key_grad, value_grad


def solution(mesh):
    return jax.shard_map(
        per_device,
        mesh=mesh,
        in_specs=(
            P(("cp", "hd"), None),
            P(("cp", "hd"), None),
            P(("cp", "hd"), None),
            P(("cp", "hd"), None),
            P(),
            P(),
        ),
        out_specs=(P("cp", "hd"), P("cp", "hd"), P("cp", "hd")),
        check_vma=False,
    )
```

time: 93.1 us -> 80.7 us (0.87)
  the two profiles are of different devices: /device:TPU:16 before, /device:TPU:24 now
where the time goes in v1:
time: 80.7 us; the launch traced here: 81.3 us
  starting transfers between devices  35.1 us (43%)
  Pallas kernels  24.6 us (30%)
  waiting for transfers between devices  15.4 us (19%)
  local copies, waits for them, and re-layouts  2.39 us (3%)
  other arithmetic  2.23 us (3%)
  between operations  1.59 us (2%)
    pallas_call x3, Pallas kernels, attention(): pl.pallas_call(functools.partial(attention_kernel, part, sums is None, en...  20.9 us
    ppermute x12, starting transfers between devices, around(): lax.ppermute(piece, 'hd', [(i, (i + shift) % 4) for i in range(4)])  18.7 us
    ppermute x3, starting transfers between devices, from_behind(): return lax.ppermute(shard, axis, pairs)  16.4 us
    ppermute x3, waiting for transfers between devices, from_behind(): return lax.ppermute(shard, axis, pairs)  9.86 us
    ppermute x12, waiting for transfers between devices, around(): lax.ppermute(piece, 'hd', [(i, (i + shift) % 4) for i in range(4)])  5.52 us
    pallas_call x1, Pallas kernels, open_cut(): pl.pallas_call(open_kernel, out_shape=tuple(shapes), in_specs=[SMEM] + [A...  3.1 us
    unnamed x14, local copies, waits for them, and re-layouts  1.62 us
  transfers between devices with their start and end apart: 15, of which 5 were waited for; matrix products, arithmetic and copies ran while one was open for 3% of the time, Pallas kernels for 26%

profile of v1, /device:TPU:24, one launch (start us, length us, event | category | flops | bytes accessed | tf_op | source)
XLA Modules:
  0.0 81.3 jit_solution(17977110292543173372)
XLA Ops:
  0.6 0.0 copy-start.6
  0.6 0.0 copy-start.3
  0.7 3.1 %open_cut.1 = (bf16[2,128,256]{2,1,0:T(8,128)(2,1)}, bf16[2,128,256]{2,1,0:T(8,128)(2,1)}, bf16[2,128,256]{2,1,0:T(8,128)(2,1)}, bf16[2,128,1024]{2,1,0:T(8,128)...) custom-call(s32[1]{0:T(128)} %bitcast.me_ref, bf16[128,1024]{1,0:T(8,128)(2,1)} %left.8, ...), custom_call_target="tpu_custom_call" | custom-call | bytes 4194304 | tf_op jit(solution)/shard_map/open_cut/pallas_call | solution.py:87
  3.8 1.6 %collective-permute-start = (bf16[2,128,256]{2,1,0:T(8,128)(2,1)}, bf16[2,128,256]{2,1,0:T(8,128)(2,1)S(1)}, u32[]{:S(2)}, u32[]{:S(2)}) collective-permute-start(bf16[2,128,256]{2,1,0:T(8,128)(2,1)} %get-tuple-element.28), channel_id=1, source_target_pairs={{0,1},{1,2},{2,3},{3,0},{4,5},{5,6},{6,7},{7,4},{8,9},{9,10},{10,1... | collective-permute-start | bytes 393224 | tf_op jit(solution)/shard_map/ppermute | solution.py:304
  5.3 1.7 %collective-permute-start.6 = (bf16[2,128,256]{2,1,0:T(8,128)(2,1)}, bf16[2,128,256]{2,1,0:T(8,128)(2,1)S(1)}, u32[]{:S(2)}, u32[]{:S(2)}) collective-permute-start(bf16[2,128,256]{2,1,0:T(8,128)(2,1)} %get-tuple-element.34), channel_id=1, source_target_pairs={{0,3},{1,0},{2,1},{3,2},{4,7},{5,4},{6,5},{7,6},{8,11},{9,8},{10,9... | collective-permute-start | bytes 393224 | tf_op jit(solution)/shard_map/ppermute | solution.py:304
  7.1 1.8 %collective-permute-start.7 = (bf16[2,128,256]{2,1,0:T(8,128)(2,1)}, bf16[2,128,256]{2,1,0:T(8,128)(2,1)S(1)}, u32[]{:S(2)}, u32[]{:S(2)}) collective-permute-start(bf16[2,128,256]{2,1,0:T(8,128)(2,1)} %get-tuple-element.35), channel_id=1, source_target_pairs={{0,2},{1,3},{2,0},{3,1},{4,6},{5,7},{6,4},{7,5},{8,10},{9,11},{10,... | collective-permute-start | bytes 393224 | tf_op jit(solution)/shard_map/ppermute | solution.py:304
  8.9 0.6 collective-permute-start.4
  9.5 2.6 %collective-permute-start.5 = (bf16[2,128,1024]{2,1,0:T(8,128)(2,1)}, bf16[2,128,1024]{2,1,0:T(8,128)(2,1)}, u32[]{:S(2)}, u32[]{:S(2)}) collective-permute-start(bf16[2,128,1024]{2,1,0:T(8,128)(2,1)} %get-tuple-element.32), channel_id=1, source_target_pairs={{0,3},{1,0},{2,1},{3,2},{4,7},{5,4},{6,5},{7,6},{8,11},{9,8},{10,9... | collective-permute-start | bytes 1572872 | tf_op jit(solution)/shard_map/ppermute | solution.py:304
  12.1 0.8 dynamic-slice_select_fusion
  12.9 0.7 dynamic_slice.10
  14.3 0.4 convert_reduce_fusion
  14.7 0.0 collective-permute-done.refs_0_.got_a
  14.7 0.0 collective-permute-done.6.got_b
  14.7 0.6 collective-permute-done.7.got_c
  15.3 1.9 %collective-permute-start.8 = (bf16[2,512,256]{2,1,0:T(8,128)(2,1)S(1)}, bf16[2,512,256]{2,1,0:T(8,128)(2,1)S(1)}, u32[]{:S(2)}, u32[]{:S(2)}) collective-permute-start(bf16[2,512,256]{2,1,0:T(8,128)(2,1)S(1)} %join.1.kv_own.refs_0_), channel_id=1, source_target_pairs={{0,4},{4,8},{8,12},{12,16},{16,20},{20,24},{24,28},{28,32},{32,36}... | collective-permute-start | bytes 1572872 | tf_op jit(solution)/shard_map/ppermute | solution.py:299
  17.3 0.1 slice.33
  17.4 1.6 %copy-done.1 = bf16[128,8192]{1,0:T(8,128)(2,1)S(1)} copy-done((bf16[128,8192]{1,0:T(8,128)(2,1)S(1)}, bf16[128,8192]{1,0:T(8,128)(2,1)}, u32[]{:S(2)}) %copy-start.1) | copy-done | bytes 2097176
  19.0 1.9 %collective-permute-start.1 = (bf16[2,128,1024]{2,1,0:T(8,128)(2,1)S(1)}, bf16[2,128,1024]{2,1,0:T(8,128)(2,1)S(1)}, u32[]{:S(2)}, u32[]{:S(2)}) collective-permute-start(bf16[2,128,1024]{2,1,0:T(8,128)(2,1)S(1)} %cut_0.1), channel_id=1, source_target_pairs={{0,2},{1,3},{2,0},{3,1},{4,6},{5,7},{6,4},{7,5},{8,10},{9,11},{10,... | collective-permute-start | bytes 1572872 | tf_op jit(solution)/shard_map/ppermute | solution.py:304
  20.9 0.0 copy-start.2
  21.0 0.9 %collective-permute-start.10 = (bf16[2,128,512]{2,1,0:T(8,128)(2,1)S(1)}, bf16[2,128,512]{2,1,0:T(8,128)(2,1)S(1)}, u32[]{:S(2)}, u32[]{:S(2)}) collective-permute-start(bf16[2,128,512]{2,1,0:T(8,128)(2,1)S(1)} %get-tuple-element.41), channel_id=1, source_target_pairs={{0,1},{1,2},{2,3},{3,0},{4,5},{5,6},{6,7},{7,4},{8,9},{9,10},{10,1... | collective-permute-start | bytes 786440 | tf_op jit(solution)/shard_map/ppermute | solution.py:304
  21.9 6.1 %collective-permute-done.8.kv_prev = bf16[2,512,256]{2,1,0:T(8,128)(2,1)S(1)} collective-permute-done((bf16[2,512,256]{2,1,0:T(8,128)(2,1)S(1)}, bf16[2,512,256]{2,1,0:T(8,128)(2,1)S(1)}, u32[]{:S(2)}, u32[]{:S(2)}) %collective-permute-start.8) | collective-permute-done | bytes 524320 | tf_op jit(solution)/shard_map/ppermute | solution.py:299
  28.0 0.4 prepare.1
  28.4 1.8 %collective-permute-start.11 = (bf16[2,128,512]{2,1,0:T(8,128)(2,1)S(1)}, bf16[2,128,512]{2,1,0:T(8,128)(2,1)S(1)}, u32[]{:S(2)}, u32[]{:S(2)}) collective-permute-start(bf16[2,128,512]{2,1,0:T(8,128)(2,1)S(1)} %get-tuple-element.42), channel_id=1, source_target_pairs={{0,3},{1,0},{2,1},{3,2},{4,7},{5,4},{6,5},{7,6},{8,11},{9,8},{10,9... | collective-permute-start | bytes 786440 | tf_op jit(solution)/shard_map/ppermute | solution.py:304
  30.3 0.0 collective-permute-done.4.refs_1_
  30.3 1.9 %collective-permute-start.12 = (bf16[2,128,512]{2,1,0:T(8,128)(2,1)S(1)}, bf16[2,128,512]{2,1,0:T(8,128)(2,1)S(1)}, u32[]{:S(2)}, u32[]{:S(2)}) collective-permute-start(bf16[2,128,512]{2,1,0:T(8,128)(2,1)S(1)} %get-tuple-element.43), channel_id=1, source_target_pairs={{0,2},{1,3},{2,0},{3,1},{4,6},{5,7},{6,4},{7,5},{8,10},{9,11},{10,... | collective-permute-start | bytes 786440 | tf_op jit(solution)/shard_map/ppermute | solution.py:304
  32.2 0.1 pad_add_fusion.1.refs_0_
  32.3 2.8 %collective-permute-done.5.refs_2_ = bf16[2,128,1024]{2,1,0:T(8,128)(2,1)} collective-permute-done((bf16[2,128,1024]{2,1,0:T(8,128)(2,1)}, bf16[2,128,1024]{2,1,0:T(8,128)(2,1)}, u32[]{:S(2)}, u32[]{:S(2)}) %collective-permute-start.5) | collective-permute-done | bytes 524320 | tf_op jit(solution)/shard_map/ppermute | solution.py:304
  35.0 2.1 %collective-permute-done.1.refs_0_.refs_3_ = bf16[2,128,1024]{2,1,0:T(8,128)(2,1)S(1)} collective-permute-done((bf16[2,128,1024]{2,1,0:T(8,128)(2,1)S(1)}, bf16[2,128,1024]{2,1,0:T(8,128)(2,1)S(1)}, u32[]{:S(2)}, u32[]{:S(2)}) %collective-permute-start.1) | collective-permute-done | bytes 524320 | tf_op jit(solution)/shard_map/ppermute | solution.py:304
  37.2 10.2 %attend_0.1 = (bf16[512,2048]{1,0:T(8,128)(2,1)}, f32[2,1024,128]{2,1,0:T(8,128)S(1)}, bf16[2,512,128]{2,1,0:T(8,128)(2,1)S(1)}) custom-call(s32[5]{0:T(128)S(1)} %pad_add_fusion.1.refs_0_, bf16[2,128,1024]{2,1,0:T(8,128)(2,1)} %collective-permute-done.4.refs_1_, bf16[2,128,1024]{2,1,0:T(8,128)(2,1)} %collective-permute-done.5.refs_2_, ...), custom_call_target="tpu_custom_call" | custom-call | flops 1677721600 | bytes 3145728 | tf_op jit(solution)/shard_map/attend_0/pallas_call | solution.py:274
  47.4 0.4 collective-permute-start.9
  47.7 0.1 cut_2.2
  47.8 2.5 %collective-permute-start.2 = (bf16[2,128,512]{2,1,0:T(8,128)(2,1)S(1)}, bf16[2,128,512]{2,1,0:T(8,128)(2,1)S(1)}, u32[]{:S(2)}, u32[]{:S(2)}) collective-permute-start(bf16[2,128,512]{2,1,0:T(8,128)(2,1)S(1)} %get-tuple-element.29), channel_id=1, source_target_pairs={{0,1},{1,2},{2,3},{3,0},{4,5},{5,6},{6,7},{7,4},{8,9},{9,10},{10,1... | collective-permute-start | bytes 786440 | tf_op jit(solution)/shard_map/ppermute | solution.py:304
  50.3 0.0 collective-permute-done.10.refs_1_
  50.3 0.9 %collective-permute-start.3 = (bf16[2,128,512]{2,1,0:T(8,128)(2,1)S(1)}, bf16[2,128,512]{2,1,0:T(8,128)(2,1)S(1)}, u32[]{:S(2)}, u32[]{:S(2)}) collective-permute-start(bf16[2,128,512]{2,1,0:T(8,128)(2,1)S(1)} %get-tuple-element.30), channel_id=1, source_target_pairs={{0,3},{1,0},{2,1},{3,2},{4,7},{5,4},{6,5},{7,6},{8,11},{9,8},{10,9... | collective-permute-start | bytes 786440 | tf_op jit(solution)/shard_map/ppermute | solution.py:304
  51.2 0.0 collective-permute-done.11.refs_2_
  51.2 0.0 collective-permute-done.12.refs_3_
  51.2 5.4 %attend_1.1 = (bf16[512,2048]{1,0:T(8,128)(2,1)}, f32[2,1024,128]{2,1,0:T(8,128)S(1)}, bf16[2,512,128]{2,1,0:T(8,128)(2,1)S(1)}) custom-call(s32[5]{0:T(128)S(1)} %pad_add_fusion.1.refs_0_, bf16[2,128,512]{2,1,0:T(8,128)(2,1)S(1)} %collective-permute-done.10.refs_1_, ...), custom_call_target="tpu_custom_call", output_to_operand_aliasing={{0}: (8, {}), {2}: (9, {})} | custom-call | flops 838860800 | bytes 1572864 | tf_op jit(solution)/shard_map/attend_1/pallas_call | solution.py:274
  56.6 8.0 %collective-permute-start.13 = (bf16[2,512,128]{2,1,0:T(8,128)(2,1)S(1)}, bf16[2,512,128]{2,1,0:T(8,128)(2,1)S(1)}, u32[]{:S(2)}, u32[]{:S(2)}) collective-permute-start(bf16[2,512,128]{2,1,0:T(8,128)(2,1)S(1)} %get-tuple-element.50), channel_id=1, source_target_pairs={{4,0},{8,4},{12,8},{16,12},{20,16},{24,20},{28,24},{32,28},{36,32}... | collective-permute-start | bytes 786440 | tf_op jit(solution)/shard_map/ppermute | solution.py:299
  64.5 0.0 collective-permute-done.9.refs_3_
  64.6 0.0 collective-permute-done.2.refs_1_
  64.6 0.0 collective-permute-done.3.refs_2_
  64.6 5.4 %attend_2.1 = (bf16[512,2048]{1,0:T(8,128)(2,1)}, f32[2,1024,128]{2,1,0:T(8,128)S(1)}, bf16[2,512,128]{2,1,0:T(8,128)(2,1)S(1)}) custom-call(s32[5]{0:T(128)S(1)} %pad_add_fusion.1.refs_0_, bf16[2,128,512]{2,1,0:T(8,128)(2,1)S(1)} %collective-permute-done.2.refs_1_, ...), custom_call_target="tpu_custom_call", output_to_operand_aliasing={{0}: (8, {})} | custom-call | flops 838860800 | bytes 1572864 | tf_op jit(solution)/shard_map/attend_2/pallas_call | solution.py:274
  70.0 6.5 %collective-permute-start.14 = (bf16[2,512,128]{2,1,0:T(8,128)(2,1)S(1)}, bf16[2,512,128]{2,1,0:T(8,128)(2,1)S(1)}, u32[]{:S(2)}, u32[]{:S(2)}) collective-permute-start(bf16[2,512,128]{2,1,0:T(8,128)(2,1)S(1)} %get-tuple-element.52), channel_id=1, source_target_pairs={{4,0},{8,4},{12,8},{16,12},{20,16},{24,20},{28,24},{32,28},{36,32}... | collective-permute-start | bytes 786440 | tf_op jit(solution)/shard_map/ppermute | solution.py:299
  76.5 0.0 collective-permute-done.13
  76.5 0.1 fusion.2
  76.6 3.8 %collective-permute-done.14 = bf16[2,512,128]{2,1,0:T(8,128)(2,1)S(1)} collective-permute-done((bf16[2,512,128]{2,1,0:T(8,128)(2,1)S(1)}, bf16[2,512,128]{2,1,0:T(8,128)(2,1)S(1)}, u32[]{:S(2)}, u32[]{:S(2)}) %collective-permute-start.14) | collective-permute-done | bytes 262176 | tf_op jit(solution)/shard_map/ppermute | solution.py:299
  80.3 0.1 fusion.3
  80.4 0.8 %pad_maximum_fusion = (bf16[512,256]{1,0:T(8,128)(2,1)}, bf16[512,256]{1,0:T(8,128)(2,1)}) fusion(bf16[512,128]{1,0:T(8,128)(2,1)S(1)} %get-tuple-element.56, bf16[512,128]{1,0:T(8,128)(2,1)S(1)} %get-tuple-element.54, bf16[512,128]{1,0:T(8,128)(2,1)S(1)} %get-tuple-element.55, bf16[512,128]{1,0:T(8,128)(2,1)S(1)} %get-tuple-element.53), kind=kLoop, calls=%fused_computation.1 | loop fusion | flops 1048576 | bytes 1048576 | tf_op jit(solution)/shard_map/concatenate | solution.py:375
  (19 shorter events, 0.3 us)
Async XLA Ops:
  0.6 12.3 %copy-start.6 = (s32[64]{0:T(128)S(1)}, s32[64]{0:T(128)}, u32[]{:S(2)}) copy-start(s32[64]{0:T(128)} %param.11) | copy-start | bytes 772
  0.6 14.6 %copy-start.3 = (bf16[128,1024]{1,0:T(8,128)(2,1)S(1)}, bf16[128,1024]{1,0:T(8,128)(2,1)}, u32[]{:S(2)}) copy-start(bf16[128,1024]{1,0:T(8,128)(2,1)} %left.8) | copy-start | bytes 786436
  0.7 14.6 %copy-start.4 = (bf16[128,1024]{1,0:T(8,128)(2,1)S(1)}, bf16[128,1024]{1,0:T(8,128)(2,1)}, u32[]{:S(2)}) copy-start(bf16[128,1024]{1,0:T(8,128)(2,1)} %right.8) | copy-start | bytes 786436
  0.7 16.7 %copy-start = (bf16[128,8192]{1,0:T(8,128)(2,1)S(1)}, bf16[128,8192]{1,0:T(8,128)(2,1)}, u32[]{:S(2)}) copy-start(bf16[128,8192]{1,0:T(8,128)(2,1)} %left.11) | copy-start | bytes 6291460
  3.8 10.9 %collective-permute-start = (bf16[2,128,256]{2,1,0:T(8,128)(2,1)}, bf16[2,128,256]{2,1,0:T(8,128)(2,1)S(1)}, u32[]{:S(2)}, u32[]{:S(2)}) collective-permute-start(bf16[2,128,256]{2,1,0:T(8,128)(2,1)} %get-tuple-element.28), channel_id=1, source_target_pairs={{0,1},{1,2},{2,3},{3,0},{4,5},{5,6},{6,7},{7,4},{8,9},{9,10},{10,1... | collective-permute-start | bytes 393224 | tf_op jit(solution)/shard_map/ppermute | solution.py:304
  5.3 9.3 %collective-permute-start.6 = (bf16[2,128,256]{2,1,0:T(8,128)(2,1)}, bf16[2,128,256]{2,1,0:T(8,128)(2,1)S(1)}, u32[]{:S(2)}, u32[]{:S(2)}) collective-permute-start(bf16[2,128,256]{2,1,0:T(8,128)(2,1)} %get-tuple-element.34), channel_id=1, source_target_pairs={{0,3},{1,0},{2,1},{3,2},{4,7},{5,4},{6,5},{7,6},{8,11},{9,8},{10,9... | collective-permute-start | bytes 393224 | tf_op jit(solution)/shard_map/ppermute | solution.py:304
  7.1 8.2 %collective-permute-start.7 = (bf16[2,128,256]{2,1,0:T(8,128)(2,1)}, bf16[2,128,256]{2,1,0:T(8,128)(2,1)S(1)}, u32[]{:S(2)}, u32[]{:S(2)}) collective-permute-start(bf16[2,128,256]{2,1,0:T(8,128)(2,1)} %get-tuple-element.35), channel_id=1, source_target_pairs={{0,2},{1,3},{2,0},{3,1},{4,6},{5,7},{6,4},{7,5},{8,10},{9,11},{10,... | collective-permute-start | bytes 393224 | tf_op jit(solution)/shard_map/ppermute | solution.py:304
  8.9 21.4 %collective-permute-start.4 = (bf16[2,128,1024]{2,1,0:T(8,128)(2,1)}, bf16[2,128,1024]{2,1,0:T(8,128)(2,1)}, u32[]{:S(2)}, u32[]{:S(2)}) collective-permute-start(bf16[2,128,1024]{2,1,0:T(8,128)(2,1)} %get-tuple-element.31), channel_id=1, source_target_pairs={{0,1},{1,2},{2,3},{3,0},{4,5},{5,6},{6,7},{7,4},{8,9},{9,10},{10,1... | collective-permute-start | bytes 1572872 | tf_op jit(solution)/shard_map/ppermute | solution.py:304
  9.5 25.5 %collective-permute-start.5 = (bf16[2,128,1024]{2,1,0:T(8,128)(2,1)}, bf16[2,128,1024]{2,1,0:T(8,128)(2,1)}, u32[]{:S(2)}, u32[]{:S(2)}) collective-permute-start(bf16[2,128,1024]{2,1,0:T(8,128)(2,1)} %get-tuple-element.32), channel_id=1, source_target_pairs={{0,3},{1,0},{2,1},{3,2},{4,7},{5,4},{6,5},{7,6},{8,11},{9,8},{10,9... | collective-permute-start | bytes 1572872 | tf_op jit(solution)/shard_map/ppermute | solution.py:304
  15.3 12.6 %collective-permute-start.8 = (bf16[2,512,256]{2,1,0:T(8,128)(2,1)S(1)}, bf16[2,512,256]{2,1,0:T(8,128)(2,1)S(1)}, u32[]{:S(2)}, u32[]{:S(2)}) collective-permute-start(bf16[2,512,256]{2,1,0:T(8,128)(2,1)S(1)} %join.1.kv_own.refs_0_), channel_id=1, source_target_pairs={{0,4},{4,8},{8,12},{12,16},{16,20},{20,24},{24,28},{28,32},{32,36}... | collective-permute-start | bytes 1572872 | tf_op jit(solution)/shard_map/ppermute | solution.py:299
  17.4 1.6 %copy-start.1 = (bf16[128,8192]{1,0:T(8,128)(2,1)S(1)}, bf16[128,8192]{1,0:T(8,128)(2,1)}, u32[]{:S(2)}) copy-start(bf16[128,8192]{1,0:T(8,128)(2,1)} %right.11) | copy-start | bytes 6291460
  19.0 18.1 %collective-permute-start.1 = (bf16[2,128,1024]{2,1,0:T(8,128)(2,1)S(1)}, bf16[2,128,1024]{2,1,0:T(8,128)(2,1)S(1)}, u32[]{:S(2)}, u32[]{:S(2)}) collective-permute-start(bf16[2,128,1024]{2,1,0:T(8,128)(2,1)S(1)} %cut_0.1), channel_id=1, source_target_pairs={{0,2},{1,3},{2,0},{3,1},{4,6},{5,7},{6,4},{7,5},{8,10},{9,11},{10,... | collective-permute-start | bytes 1572872 | tf_op jit(solution)/shard_map/ppermute | solution.py:304
  20.9 7.5 %copy-start.2 = (bf16[128,8192]{1,0:T(8,128)(2,1)S(1)}, bf16[128,8192]{1,0:T(8,128)(2,1)}, u32[]{:S(2)}) copy-start(bf16[128,8192]{1,0:T(8,128)(2,1)} %right.11) | copy-start | bytes 6291460
  21.0 29.3 %collective-permute-start.10 = (bf16[2,128,512]{2,1,0:T(8,128)(2,1)S(1)}, bf16[2,128,512]{2,1,0:T(8,128)(2,1)S(1)}, u32[]{:S(2)}, u32[]{:S(2)}) collective-permute-start(bf16[2,128,512]{2,1,0:T(8,128)(2,1)S(1)} %get-tuple-element.41), channel_id=1, source_target_pairs={{0,1},{1,2},{2,3},{3,0},{4,5},{5,6},{6,7},{7,4},{8,9},{9,10},{10,1... | collective-permute-start | bytes 786440 | tf_op jit(solution)/shard_map/ppermute | solution.py:304
  28.4 8.8 %copy-start.5 = (bf16[2,128,1024]{2,1,0:T(8,128)(2,1)S(1)}, bf16[2,128,1024]{2,1,0:T(8,128)(2,1)}, u32[]{:S(2)}) copy-start(bf16[2,128,1024]{2,1,0:T(8,128)(2,1)} %get-tuple-element.33.refs_4_) | copy-start | bytes 1572868
  28.4 22.8 %collective-permute-start.11 = (bf16[2,128,512]{2,1,0:T(8,128)(2,1)S(1)}, bf16[2,128,512]{2,1,0:T(8,128)(2,1)S(1)}, u32[]{:S(2)}, u32[]{:S(2)}) collective-permute-start(bf16[2,128,512]{2,1,0:T(8,128)(2,1)S(1)} %get-tuple-element.42), channel_id=1, source_target_pairs={{0,3},{1,0},{2,1},{3,2},{4,7},{5,4},{6,5},{7,6},{8,11},{9,8},{10,9... | collective-permute-start | bytes 786440 | tf_op jit(solution)/shard_map/ppermute | solution.py:304
  30.3 20.9 %collective-permute-start.12 = (bf16[2,128,512]{2,1,0:T(8,128)(2,1)S(1)}, bf16[2,128,512]{2,1,0:T(8,128)(2,1)S(1)}, u32[]{:S(2)}, u32[]{:S(2)}) collective-permute-start(bf16[2,128,512]{2,1,0:T(8,128)(2,1)S(1)} %get-tuple-element.43), channel_id=1, source_target_pairs={{0,2},{1,3},{2,0},{3,1},{4,6},{5,7},{6,4},{7,5},{8,10},{9,11},{10,... | collective-permute-start | bytes 786440 | tf_op jit(solution)/shard_map/ppermute | solution.py:304
  47.4 17.2 %collective-permute-start.9 = (bf16[2,128,512]{2,1,0:T(8,128)(2,1)S(1)}, bf16[2,128,512]{2,1,0:T(8,128)(2,1)S(1)}, u32[]{:S(2)}, u32[]{:S(2)}) collective-permute-start(bf16[2,128,512]{2,1,0:T(8,128)(2,1)S(1)} %cut_2.3), channel_id=1, source_target_pairs={{0,2},{1,3},{2,0},{3,1},{4,6},{5,7},{6,4},{7,5},{8,10},{9,11},{10,... | collective-permute-start | bytes 786440 | tf_op jit(solution)/shard_map/ppermute | solution.py:304
  47.8 16.8 %collective-permute-start.2 = (bf16[2,128,512]{2,1,0:T(8,128)(2,1)S(1)}, bf16[2,128,512]{2,1,0:T(8,128)(2,1)S(1)}, u32[]{:S(2)}, u32[]{:S(2)}) collective-permute-start(bf16[2,128,512]{2,1,0:T(8,128)(2,1)S(1)} %get-tuple-element.29), channel_id=1, source_target_pairs={{0,1},{1,2},{2,3},{3,0},{4,5},{5,6},{6,7},{7,4},{8,9},{9,10},{10,1... | collective-permute-start | bytes 786440 | tf_op jit(solution)/shard_map/ppermute | solution.py:304
  50.3 14.3 %collective-permute-start.3 = (bf16[2,128,512]{2,1,0:T(8,128)(2,1)S(1)}, bf16[2,128,512]{2,1,0:T(8,128)(2,1)S(1)}, u32[]{:S(2)}, u32[]{:S(2)}) collective-permute-start(bf16[2,128,512]{2,1,0:T(8,128)(2,1)S(1)} %get-tuple-element.30), channel_id=1, source_target_pairs={{0,3},{1,0},{2,1},{3,2},{4,7},{5,4},{6,5},{7,6},{8,11},{9,8},{10,9... | collective-permute-start | bytes 786440 | tf_op jit(solution)/shard_map/ppermute | solution.py:304
  56.6 19.9 %collective-permute-start.13 = (bf16[2,512,128]{2,1,0:T(8,128)(2,1)S(1)}, bf16[2,512,128]{2,1,0:T(8,128)(2,1)S(1)}, u32[]{:S(2)}, u32[]{:S(2)}) collective-permute-start(bf16[2,512,128]{2,1,0:T(8,128)(2,1)S(1)} %get-tuple-element.50), channel_id=1, source_target_pairs={{4,0},{8,4},{12,8},{16,12},{20,16},{24,20},{28,24},{32,28},{36,32}... | collective-permute-start | bytes 786440 | tf_op jit(solution)/shard_map/ppermute | solution.py:299
  70.0 10.4 %collective-permute-start.14 = (bf16[2,512,128]{2,1,0:T(8,128)(2,1)S(1)}, bf16[2,512,128]{2,1,0:T(8,128)(2,1)S(1)}, u32[]{:S(2)}, u32[]{:S(2)}) collective-permute-start(bf16[2,512,128]{2,1,0:T(8,128)(2,1)S(1)} %get-tuple-element.52), channel_id=1, source_target_pairs={{4,0},{8,4},{12,8},{16,12},{20,16},{24,20},{28,24},{32,28},{36,32}... | collective-permute-start | bytes 786440 | tf_op jit(solution)/shard_map/ppermute | solution.py:299

commit v2 on v1

--- a/solution.py
+++ b/solution.py
@@ -10,7 +10,6 @@
 
 HEAD_DIM = 128
 TILE = 128
-STACK = 4
 SHIFTS = (1, -1, 2)
 SENT = ((0, 8), (8, 4), (12, 4))
 PARTS = ((0, 0, 8, 0), (1, 0, 4, 1), (1, 4, 4, 2))
@@ -160,8 +159,8 @@
 def attention_kernel(part, begins, ends, passes, *refs):
     group, first, heads, sent = part
     offset = group * 8 + first - SENT[sent][0]
-    stacks = heads // STACK
-    wide = STACK * HEAD_DIM
+    stacks = 1
+    wide = heads * HEAD_DIM
     refs = list(refs)
     scal, *pieces, kv, keys_t, bias = refs[:8]
     refs = refs[8 + (first + group > 0) :]
@@ -178,8 +177,8 @@
     for shift, piece in zip((*SHIFTS, 0), pieces):
         row = source_of(me, shift)
         for stack in range(stacks):
-            for h in range(STACK):
-                head = offset + stack * STACK + h
+            for h in range(heads):
+                head = offset + stack * heads + h
                 columns = slice(head * HEAD_DIM, (head + 1) * HEAD_DIM)
                 at = slice(h * TILE, (h + 1) * TILE)
                 q_all[stack, row, at, :] = piece[0, :, columns]
@@ -198,7 +197,7 @@
         key, value = kv[0, window, lanes], kv[1, window, lanes]
         q, d = q_all[stack, row], d_all[stack, row]
         mask = bias[row, (5 - tiles) * TILE :, :]
-        scores = dot(key, q, ROWS_BY_ROWS) * to_exponent + jnp.concatenate([mask] * STACK, axis=1)
+        scores = dot(key, q, ROWS_BY_ROWS) * to_exponent + jnp.concatenate([mask] * heads, axis=1)
         highest = jnp.max(scores, axis=0, keepdims=True)
         weights = jnp.exp2(scores - highest)
         probs = weights * (1.0 / jnp.sum(weights, axis=0, keepdims=True))
@@ -210,13 +209,13 @@
         key_t = jnp.concatenate([keys_t[group, tile + i] for i in range(tiles)], axis=1)
         dq_t = dot(key_t, dscores, ROWS_BY_COLUMNS) * scale
         own = pl.ds(aligned(row, TILE), TILE)
-        for h in range(STACK):
+        for h in range(heads):
             columns = slice(h * HEAD_DIM, (h + 1) * HEAD_DIM)
             dq[stack, own, columns] = dq_t[:, columns].T.astype(jnp.bfloat16)
 
     def out_copy(stack, row):
         own = pl.ds(aligned(row, TILE), TILE)
-        column = (group * 8 + first + stack * STACK) * HEAD_DIM
+        column = (group * 8 + first + stack * heads) * HEAD_DIM
         return pltpu.make_async_copy(
             dq.at[stack, own, :],
             query_out.at[own, pl.ds(column, wide)],
@@ -248,8 +247,8 @@
     group, first, heads, sent = part
     rows = pieces[0].shape[1]
     block = 4 * rows
-    stacks = heads // STACK
-    wide = STACK * HEAD_DIM
+    stacks = 1
+    wide = heads * HEAD_DIM
     args = [scal, *pieces, *ready]
     specs = [SMEM] + [VMEM] * 7
     shapes = [jax.ShapeDtypeStruct((block, 2048), jnp.bfloat16)]
@@ -277,8 +276,8 @@
         in_specs=specs,
         out_specs=tuple(out_specs),
         scratch_shapes=[
-            pltpu.VMEM((stacks, 4, STACK * TILE, HEAD_DIM), jnp.bfloat16),
-            pltpu.VMEM((stacks, 4, STACK * TILE, HEAD_DIM), jnp.bfloat16),
+            pltpu.VMEM((stacks, 4, heads * TILE, HEAD_DIM), jnp.bfloat16),
+            pltpu.VMEM((stacks, 4, heads * TILE, HEAD_DIM), jnp.bfloat16),
             pltpu.VMEM((stacks, block, wide), jnp.bfloat16),
             pltpu.SemaphoreType.DMA((stacks, 4)),
         ],
@@ -338,10 +337,9 @@
 
     *sent, own_a = opened[3:]
     sent_a = [*sent, *cut_heads(0, (2,), got_kv[:1])]
-    sent, own_b = cut_heads(1, (1, 0), (kv_own,))
-    sent_b = [sent, *cut_heads(1, (-1, 2), ready)]
+    *sent_b, own_b = cut_heads(1, (1, -1, 2, 0), ready)
     got_a = around(sent_a)
-    *sent_c, own_c = cut_heads(2, (1, -1, 0), got_a[2:])
+    *sent_c, own_c = cut_heads(2, (1, -1, 0), got_a[:1])
     pieces = [[*got_a, own_a], [*around(sent_b), own_b]]
 
     query_grad, sums, passed = None, None, []

time: 80.7 us -> 77.4 us (0.959); the launches traced: 81.3 us -> 76.5 us
  Pallas kernels: 24.6 us -> 21.1 us
  starting transfers between devices: 35.1 us -> 33 us
  waiting for transfers between devices: 15.4 us -> 16.4 us
    pallas_call x3, Pallas kernels: 20.9 us -> 17.4 us  [attention(): pl.pallas_call(functools.partial(attention_kernel, part, sums is None, en...]
    ppermute x3, starting transfers between devices: 16.4 us -> 15.3 us  [from_behind(): return lax.ppermute(shard, axis, pairs)]
    ppermute x3, waiting for transfers between devices: 9.86 us -> 10.9 us  [from_behind(): return lax.ppermute(shard, axis, pairs)]
    ppermute x12, starting transfers between devices: 18.7 us -> 17.7 us  [around(): lax.ppermute(piece, 'hd', [(i, (i + shift) % 4) for i in range(4)])]
  transfers between devices with their start and end apart: 15 -> 15, of which waited for: 5 -> 5; matrix products, arithmetic and copies ran while one was open for 3% -> 3% of each run, Pallas kernels for 26% -> 24%
where the time goes in v2:
time: 77.4 us; the launch traced here: 76.5 us
  starting transfers between devices  33 us (43%)
  Pallas kernels  21.1 us (27%)
  waiting for transfers between devices  16.4 us (21%)
  local copies, waits for them, and re-layouts  2.31 us (3%)
  other arithmetic  2.22 us (3%)
  between operations  1.46 us (2%)
    ppermute x12, starting transfers between devices, around(): lax.ppermute(piece, 'hd', [(i, (i + shift) % 4) for i in range(4)])  17.7 us
    pallas_call x3, Pallas kernels, attention(): pl.pallas_call(functools.partial(attention_kernel, part, sums is None, en...  17.4 us
    ppermute x3, starting transfers between devices, from_behind(): return lax.ppermute(shard, axis, pairs)  15.3 us
    ppermute x3, waiting for transfers between devices, from_behind(): return lax.ppermute(shard, axis, pairs)  10.9 us
    ppermute x12, waiting for transfers between devices, around(): lax.ppermute(piece, 'hd', [(i, (i + shift) % 4) for i in range(4)])  5.53 us
    pallas_call x1, Pallas kernels, open_cut(): pl.pallas_call(open_kernel, out_shape=tuple(shapes), in_specs=[SMEM] + [A...  3.08 us
    unnamed x14, local copies, waits for them, and re-layouts  1.62 us
  transfers between devices with their start and end apart: 15, of which 5 were waited for; matrix products, arithmetic and copies ran while one was open for 3% of the time, Pallas kernels for 24%

profile of v2, /device:TPU:24, one launch (start us, length us, event | category | flops | bytes accessed | tf_op | source)
XLA Modules:
  0.0 76.5 jit_solution(10869839107262379362)
XLA Ops:
  0.6 0.0 copy-start.6
  0.6 0.0 copy-start.3
  0.7 3.1 %open_cut.1 = (bf16[2,128,256]{2,1,0:T(8,128)(2,1)}, bf16[2,128,256]{2,1,0:T(8,128)(2,1)}, bf16[2,128,256]{2,1,0:T(8,128)(2,1)}, bf16[2,128,1024]{2,1,0:T(8,128)...) custom-call(s32[1]{0:T(128)} %bitcast.me_ref, bf16[128,1024]{1,0:T(8,128)(2,1)} %left.7, ...), custom_call_target="tpu_custom_call" | custom-call | bytes 4194304 | tf_op jit(solution)/shard_map/open_cut/pallas_call | solution.py:86
  3.8 1.6 %collective-permute-start.4 = (bf16[2,128,256]{2,1,0:T(8,128)(2,1)}, bf16[2,128,256]{2,1,0:T(8,128)(2,1)S(1)}, u32[]{:S(2)}, u32[]{:S(2)}) collective-permute-start(bf16[2,128,256]{2,1,0:T(8,128)(2,1)} %get-tuple-element.32), channel_id=1, source_target_pairs={{0,1},{1,2},{2,3},{3,0},{4,5},{5,6},{6,7},{7,4},{8,9},{9,10},{10,1... | collective-permute-start | bytes 393224 | tf_op jit(solution)/shard_map/ppermute | solution.py:303
  5.3 1.7 %collective-permute-start.6 = (bf16[2,128,256]{2,1,0:T(8,128)(2,1)}, bf16[2,128,256]{2,1,0:T(8,128)(2,1)S(1)}, u32[]{:S(2)}, u32[]{:S(2)}) collective-permute-start(bf16[2,128,256]{2,1,0:T(8,128)(2,1)} %get-tuple-element.34), channel_id=1, source_target_pairs={{0,3},{1,0},{2,1},{3,2},{4,7},{5,4},{6,5},{7,6},{8,11},{9,8},{10,9... | collective-permute-start | bytes 393224 | tf_op jit(solution)/shard_map/ppermute | solution.py:303
  7.1 1.8 %collective-permute-start.7 = (bf16[2,128,256]{2,1,0:T(8,128)(2,1)}, bf16[2,128,256]{2,1,0:T(8,128)(2,1)S(1)}, u32[]{:S(2)}, u32[]{:S(2)}) collective-permute-start(bf16[2,128,256]{2,1,0:T(8,128)(2,1)} %get-tuple-element.35), channel_id=1, source_target_pairs={{0,2},{1,3},{2,0},{3,1},{4,6},{5,7},{6,4},{7,5},{8,10},{9,11},{10,... | collective-permute-start | bytes 393224 | tf_op jit(solution)/shard_map/ppermute | solution.py:303
  8.9 0.6 collective-permute-start
  9.5 2.6 %collective-permute-start.3 = (bf16[2,128,1024]{2,1,0:T(8,128)(2,1)}, bf16[2,128,1024]{2,1,0:T(8,128)(2,1)}, u32[]{:S(2)}, u32[]{:S(2)}) collective-permute-start(bf16[2,128,1024]{2,1,0:T(8,128)(2,1)} %get-tuple-element.31), channel_id=1, source_target_pairs={{0,3},{1,0},{2,1},{3,2},{4,7},{5,4},{6,5},{7,6},{8,11},{9,8},{10,9... | collective-permute-start | bytes 1572872 | tf_op jit(solution)/shard_map/ppermute | solution.py:303
  12.1 0.8 %dynamic-slice_select_fusion = (s32[512]{0:T(512)S(1)}, s32[512]{0:T(512)S(1)}) fusion(s32[32768]{0:T(1024)} %param.10, s32[]{:T(128)S(6)} %select_n.45, pred[]{:T(512)S(6)} %gt.3, s32[]{:T(128)S(6)} %select_n.47), kind=kLoop, calls=%fused_computation.14 | loop fusion | flops 512 | bytes 8201 | tf_op jit(solution)/shard_map/jit(_where)/select_n | solution.py:323
  12.9 0.6 dynamic_slice.10
  14.1 0.4 convert_reduce_fusion
  14.5 0.0 collective-permute-done.4.refs_0_.got_a
  14.5 0.0 collective-permute-done.6.got_b
  14.5 0.8 %collective-permute-done.7.got_c = bf16[2,128,256]{2,1,0:T(8,128)(2,1)S(1)} collective-permute-done((bf16[2,128,256]{2,1,0:T(8,128)(2,1)}, bf16[2,128,256]{2,1,0:T(8,128)(2,1)S(1)}, u32[]{:S(2)}, u32[]{:S(2)}) %collective-permute-start.7) | collective-permute-done | bytes 131104 | tf_op jit(solution)/shard_map/ppermute | solution.py:303
  15.3 1.9 %collective-permute-start.8 = (bf16[2,512,256]{2,1,0:T(8,128)(2,1)S(1)}, bf16[2,512,256]{2,1,0:T(8,128)(2,1)S(1)}, u32[]{:S(2)}, u32[]{:S(2)}) collective-permute-start(bf16[2,512,256]{2,1,0:T(8,128)(2,1)S(1)} %join.1.kv_own), channel_id=1, source_target_pairs={{0,4},{4,8},{8,12},{12,16},{16,20},{20,24},{24,28},{28,32},{32,36}... | collective-permute-start | bytes 1572872 | tf_op jit(solution)/shard_map/ppermute | solution.py:298
  17.3 0.1 slice.33
  17.4 1.6 %copy-done.1 = bf16[128,8192]{1,0:T(8,128)(2,1)S(1)} copy-done((bf16[128,8192]{1,0:T(8,128)(2,1)S(1)}, bf16[128,8192]{1,0:T(8,128)(2,1)}, u32[]{:S(2)}) %copy-start.1) | copy-done | bytes 2097176
  19.0 1.9 %collective-permute-start.5 = (bf16[2,128,1024]{2,1,0:T(8,128)(2,1)S(1)}, bf16[2,128,1024]{2,1,0:T(8,128)(2,1)S(1)}, u32[]{:S(2)}, u32[]{:S(2)}) collective-permute-start(bf16[2,128,1024]{2,1,0:T(8,128)(2,1)S(1)} %cut_0.1), channel_id=1, source_target_pairs={{0,2},{1,3},{2,0},{3,1},{4,6},{5,7},{6,4},{7,5},{8,10},{9,11},{10,... | collective-permute-start | bytes 1572872 | tf_op jit(solution)/shard_map/ppermute | solution.py:303
  20.9 7.1 %collective-permute-done.8.kv_prev = bf16[2,512,256]{2,1,0:T(8,128)(2,1)S(1)} collective-permute-done((bf16[2,512,256]{2,1,0:T(8,128)(2,1)S(1)}, bf16[2,512,256]{2,1,0:T(8,128)(2,1)S(1)}, u32[]{:S(2)}, u32[]{:S(2)}) %collective-permute-start.8) | collective-permute-done | bytes 524320 | tf_op jit(solution)/shard_map/ppermute | solution.py:298
  28.0 0.4 prepare.1
  28.4 0.1 cut_1.1
  28.5 1.7 %collective-permute-start.10 = (bf16[2,128,512]{2,1,0:T(8,128)(2,1)S(1)}, bf16[2,128,512]{2,1,0:T(8,128)(2,1)S(1)}, u32[]{:S(2)}, u32[]{:S(2)}) collective-permute-start(bf16[2,128,512]{2,1,0:T(8,128)(2,1)S(1)} %get-tuple-element.41), channel_id=1, source_target_pairs={{0,1},{1,2},{2,3},{3,0},{4,5},{5,6},{6,7},{7,4},{8,9},{9,10},{10,1... | collective-permute-start | bytes 786440 | tf_op jit(solution)/shard_map/ppermute | solution.py:303
  30.1 1.6 %collective-permute-start.11 = (bf16[2,128,512]{2,1,0:T(8,128)(2,1)S(1)}, bf16[2,128,512]{2,1,0:T(8,128)(2,1)S(1)}, u32[]{:S(2)}, u32[]{:S(2)}) collective-permute-start(bf16[2,128,512]{2,1,0:T(8,128)(2,1)S(1)} %get-tuple-element.42), channel_id=1, source_target_pairs={{0,3},{1,0},{2,1},{3,2},{4,7},{5,4},{6,5},{7,6},{8,11},{9,8},{10,9... | collective-permute-start | bytes 786440 | tf_op jit(solution)/shard_map/ppermute | solution.py:303
  31.8 0.0 collective-permute-done.refs_0_.refs_1_
  31.8 0.5 collective-permute-start.12
  32.3 0.1 pad_add_fusion.1.refs_0_
  32.4 0.1 cut_2.2
  32.5 2.6 %collective-permute-done.3.refs_2_ = bf16[2,128,1024]{2,1,0:T(8,128)(2,1)} collective-permute-done((bf16[2,128,1024]{2,1,0:T(8,128)(2,1)}, bf16[2,128,1024]{2,1,0:T(8,128)(2,1)}, u32[]{:S(2)}, u32[]{:S(2)}) %collective-permute-start.3) | collective-permute-done | bytes 524320 | tf_op jit(solution)/shard_map/ppermute | solution.py:303
  35.0 0.0 collective-permute-start.1
  35.0 2.1 %collective-permute-done.5.refs_3_ = bf16[2,128,1024]{2,1,0:T(8,128)(2,1)S(1)} collective-permute-done((bf16[2,128,1024]{2,1,0:T(8,128)(2,1)S(1)}, bf16[2,128,1024]{2,1,0:T(8,128)(2,1)S(1)}, u32[]{:S(2)}, u32[]{:S(2)}) %collective-permute-start.5) | collective-permute-done | bytes 524320 | tf_op jit(solution)/shard_map/ppermute | solution.py:303
  37.1 1.8 %collective-permute-start.2 = (bf16[2,128,512]{2,1,0:T(8,128)(2,1)S(1)}, bf16[2,128,512]{2,1,0:T(8,128)(2,1)S(1)}, u32[]{:S(2)}, u32[]{:S(2)}) collective-permute-start(bf16[2,128,512]{2,1,0:T(8,128)(2,1)S(1)} %get-tuple-element.30), channel_id=1, source_target_pairs={{0,3},{1,0},{2,1},{3,2},{4,7},{5,4},{6,5},{7,6},{8,11},{9,8},{10,9... | collective-permute-start | bytes 786440 | tf_op jit(solution)/shard_map/ppermute | solution.py:303
  39.0 7.6 %attend_0.1 = (bf16[512,2048]{1,0:T(8,128)(2,1)}, f32[2,1024,128]{2,1,0:T(8,128)S(1)}, bf16[2,512,128]{2,1,0:T(8,128)(2,1)S(1)}) custom-call(s32[5]{0:T(128)S(1)} %pad_add_fusion.1.refs_0_, bf16[2,128,1024]{2,1,0:T(8,128)(2,1)} %collective-permute-done.refs_0_.refs_1_, bf16[2,128,1024]{2,1,0:T(8,128)(2,1)} %collective-permute-done.3.refs_2_, ...), custom_call_target="tpu_custom_call" | custom-call | flops 1677721600 | bytes 3145728 | tf_op jit(solution)/shard_map/attend_0/pallas_call | solution.py:273
  46.6 0.0 collective-permute-done.10.refs_1_
  46.6 1.8 %collective-permute-start.9 = (bf16[2,128,512]{2,1,0:T(8,128)(2,1)S(1)}, bf16[2,128,512]{2,1,0:T(8,128)(2,1)S(1)}, u32[]{:S(2)}, u32[]{:S(2)}) collective-permute-start(bf16[2,128,512]{2,1,0:T(8,128)(2,1)S(1)} %cut_2.3), channel_id=1, source_target_pairs={{0,2},{1,3},{2,0},{3,1},{4,6},{5,7},{6,4},{7,5},{8,10},{9,11},{10,... | collective-permute-start | bytes 786440 | tf_op jit(solution)/shard_map/ppermute | solution.py:303
  48.4 0.0 collective-permute-done.11.refs_2_
  48.4 0.0 collective-permute-done.12.refs_3_
  48.4 4.9 %attend_1.1 = (bf16[512,2048]{1,0:T(8,128)(2,1)}, f32[2,1024,128]{2,1,0:T(8,128)S(1)}, bf16[2,512,128]{2,1,0:T(8,128)(2,1)S(1)}) custom-call(s32[5]{0:T(128)S(1)} %pad_add_fusion.1.refs_0_, bf16[2,128,512]{2,1,0:T(8,128)(2,1)S(1)} %collective-permute-done.10.refs_1_, ...), custom_call_target="tpu_custom_call", output_to_operand_aliasing={{0}: (8, {}), {2}: (9, {})} | custom-call | flops 838860800 | bytes 1572864 | tf_op jit(solution)/shard_map/attend_1/pallas_call | solution.py:273
  53.3 7.3 %collective-permute-start.13 = (bf16[2,512,128]{2,1,0:T(8,128)(2,1)S(1)}, bf16[2,512,128]{2,1,0:T(8,128)(2,1)S(1)}, u32[]{:S(2)}, u32[]{:S(2)}) collective-permute-start(bf16[2,512,128]{2,1,0:T(8,128)(2,1)S(1)} %get-tuple-element.50), channel_id=1, source_target_pairs={{4,0},{8,4},{12,8},{16,12},{20,16},{24,20},{28,24},{32,28},{36,32}... | collective-permute-start | bytes 786440 | tf_op jit(solution)/shard_map/ppermute | solution.py:298
  60.7 0.0 collective-permute-done.1.refs_1_
  60.7 0.0 collective-permute-done.2.refs_2_
  60.7 0.0 collective-permute-done.9.refs_3_
  60.7 4.9 %attend_2.1 = (bf16[512,2048]{1,0:T(8,128)(2,1)}, f32[2,1024,128]{2,1,0:T(8,128)S(1)}, bf16[2,512,128]{2,1,0:T(8,128)(2,1)S(1)}) custom-call(s32[5]{0:T(128)S(1)} %pad_add_fusion.1.refs_0_, bf16[2,128,512]{2,1,0:T(8,128)(2,1)S(1)} %collective-permute-done.1.refs_1_, ...), custom_call_target="tpu_custom_call", output_to_operand_aliasing={{0}: (8, {})} | custom-call | flops 838860800 | bytes 1572864 | tf_op jit(solution)/shard_map/attend_2/pallas_call | solution.py:273
  65.7 6.0 %collective-permute-start.14 = (bf16[2,512,128]{2,1,0:T(8,128)(2,1)S(1)}, bf16[2,512,128]{2,1,0:T(8,128)(2,1)S(1)}, u32[]{:S(2)}, u32[]{:S(2)}) collective-permute-start(bf16[2,512,128]{2,1,0:T(8,128)(2,1)S(1)} %get-tuple-element.52), channel_id=1, source_target_pairs={{4,0},{8,4},{12,8},{16,12},{20,16},{24,20},{28,24},{32,28},{36,32}... | collective-permute-start | bytes 786440 | tf_op jit(solution)/shard_map/ppermute | solution.py:298
  71.7 0.0 collective-permute-done.13
  71.7 0.1 fusion.2
  71.8 3.8 %collective-permute-done.14 = bf16[2,512,128]{2,1,0:T(8,128)(2,1)S(1)} collective-permute-done((bf16[2,512,128]{2,1,0:T(8,128)(2,1)S(1)}, bf16[2,512,128]{2,1,0:T(8,128)(2,1)S(1)}, u32[]{:S(2)}, u32[]{:S(2)}) %collective-permute-start.14) | collective-permute-done | bytes 262176 | tf_op jit(solution)/shard_map/ppermute | solution.py:298
  75.6 0.1 fusion.3
  75.6 0.8 %pad_maximum_fusion = (bf16[512,256]{1,0:T(8,128)(2,1)}, bf16[512,256]{1,0:T(8,128)(2,1)}) fusion(bf16[512,128]{1,0:T(8,128)(2,1)S(1)} %get-tuple-element.56, bf16[512,128]{1,0:T(8,128)(2,1)S(1)} %get-tuple-element.54, bf16[512,128]{1,0:T(8,128)(2,1)S(1)} %get-tuple-element.55, bf16[512,128]{1,0:T(8,128)(2,1)S(1)} %get-tuple-element.53), kind=kLoop, calls=%fused_computation.1 | loop fusion | flops 1048576 | bytes 1048576 | tf_op jit(solution)/shard_map/concatenate | solution.py:373
  (18 shorter events, 0.2 us)
Async XLA Ops:
  0.6 12.3 %copy-start.6 = (s32[64]{0:T(128)S(1)}, s32[64]{0:T(128)}, u32[]{:S(2)}) copy-start(s32[64]{0:T(128)} %param.11) | copy-start | bytes 772
  0.6 14.6 %copy-start.3 = (bf16[128,1024]{1,0:T(8,128)(2,1)S(1)}, bf16[128,1024]{1,0:T(8,128)(2,1)}, u32[]{:S(2)}) copy-start(bf16[128,1024]{1,0:T(8,128)(2,1)} %left.7) | copy-start | bytes 786436
  0.7 14.6 %copy-start.4 = (bf16[128,1024]{1,0:T(8,128)(2,1)S(1)}, bf16[128,1024]{1,0:T(8,128)(2,1)}, u32[]{:S(2)}) copy-start(bf16[128,1024]{1,0:T(8,128)(2,1)} %right.7) | copy-start | bytes 786436
  0.7 16.7 %copy-start = (bf16[128,8192]{1,0:T(8,128)(2,1)S(1)}, bf16[128,8192]{1,0:T(8,128)(2,1)}, u32[]{:S(2)}) copy-start(bf16[128,8192]{1,0:T(8,128)(2,1)} %left.9) | copy-start | bytes 6291460
  3.8 10.7 %collective-permute-start.4 = (bf16[2,128,256]{2,1,0:T(8,128)(2,1)}, bf16[2,128,256]{2,1,0:T(8,128)(2,1)S(1)}, u32[]{:S(2)}, u32[]{:S(2)}) collective-permute-start(bf16[2,128,256]{2,1,0:T(8,128)(2,1)} %get-tuple-element.32), channel_id=1, source_target_pairs={{0,1},{1,2},{2,3},{3,0},{4,5},{5,6},{6,7},{7,4},{8,9},{9,10},{10,1... | collective-permute-start | bytes 393224 | tf_op jit(solution)/shard_map/ppermute | solution.py:303
  5.3 9.1 %collective-permute-start.6 = (bf16[2,128,256]{2,1,0:T(8,128)(2,1)}, bf16[2,128,256]{2,1,0:T(8,128)(2,1)S(1)}, u32[]{:S(2)}, u32[]{:S(2)}) collective-permute-start(bf16[2,128,256]{2,1,0:T(8,128)(2,1)} %get-tuple-element.34), channel_id=1, source_target_pairs={{0,3},{1,0},{2,1},{3,2},{4,7},{5,4},{6,5},{7,6},{8,11},{9,8},{10,9... | collective-permute-start | bytes 393224 | tf_op jit(solution)/shard_map/ppermute | solution.py:303
  7.1 8.2 %collective-permute-start.7 = (bf16[2,128,256]{2,1,0:T(8,128)(2,1)}, bf16[2,128,256]{2,1,0:T(8,128)(2,1)S(1)}, u32[]{:S(2)}, u32[]{:S(2)}) collective-permute-start(bf16[2,128,256]{2,1,0:T(8,128)(2,1)} %get-tuple-element.35), channel_id=1, source_target_pairs={{0,2},{1,3},{2,0},{3,1},{4,6},{5,7},{6,4},{7,5},{8,10},{9,11},{10,... | collective-permute-start | bytes 393224 | tf_op jit(solution)/shard_map/ppermute | solution.py:303
  8.9 22.9 %collective-permute-start = (bf16[2,128,1024]{2,1,0:T(8,128)(2,1)}, bf16[2,128,1024]{2,1,0:T(8,128)(2,1)}, u32[]{:S(2)}, u32[]{:S(2)}) collective-permute-start(bf16[2,128,1024]{2,1,0:T(8,128)(2,1)} %get-tuple-element.28), channel_id=1, source_target_pairs={{0,1},{1,2},{2,3},{3,0},{4,5},{5,6},{6,7},{7,4},{8,9},{9,10},{10,1... | collective-permute-start | bytes 1572872 | tf_op jit(solution)/shard_map/ppermute | solution.py:303
  9.5 25.5 %collective-permute-start.3 = (bf16[2,128,1024]{2,1,0:T(8,128)(2,1)}, bf16[2,128,1024]{2,1,0:T(8,128)(2,1)}, u32[]{:S(2)}, u32[]{:S(2)}) collective-permute-start(bf16[2,128,1024]{2,1,0:T(8,128)(2,1)} %get-tuple-element.31), channel_id=1, source_target_pairs={{0,3},{1,0},{2,1},{3,2},{4,7},{5,4},{6,5},{7,6},{8,11},{9,8},{10,9... | collective-permute-start | bytes 1572872 | tf_op jit(solution)/shard_map/ppermute | solution.py:303
  15.3 12.6 %collective-permute-start.8 = (bf16[2,512,256]{2,1,0:T(8,128)(2,1)S(1)}, bf16[2,512,256]{2,1,0:T(8,128)(2,1)S(1)}, u32[]{:S(2)}, u32[]{:S(2)}) collective-permute-start(bf16[2,512,256]{2,1,0:T(8,128)(2,1)S(1)} %join.1.kv_own), channel_id=1, source_target_pairs={{0,4},{4,8},{8,12},{12,16},{16,20},{20,24},{24,28},{28,32},{32,36}... | collective-permute-start | bytes 1572872 | tf_op jit(solution)/shard_map/ppermute | solution.py:298
  17.4 1.6 %copy-start.1 = (bf16[128,8192]{1,0:T(8,128)(2,1)S(1)}, bf16[128,8192]{1,0:T(8,128)(2,1)}, u32[]{:S(2)}) copy-start(bf16[128,8192]{1,0:T(8,128)(2,1)} %right.9) | copy-start | bytes 6291460
  19.0 9.4 %copy-start.2 = (bf16[128,8192]{1,0:T(8,128)(2,1)S(1)}, bf16[128,8192]{1,0:T(8,128)(2,1)}, u32[]{:S(2)}) copy-start(bf16[128,8192]{1,0:T(8,128)(2,1)} %right.9) | copy-start | bytes 6291460
  19.0 18.1 %collective-permute-start.5 = (bf16[2,128,1024]{2,1,0:T(8,128)(2,1)S(1)}, bf16[2,128,1024]{2,1,0:T(8,128)(2,1)S(1)}, u32[]{:S(2)}, u32[]{:S(2)}) collective-permute-start(bf16[2,128,1024]{2,1,0:T(8,128)(2,1)S(1)} %cut_0.1), channel_id=1, source_target_pairs={{0,2},{1,3},{2,0},{3,1},{4,6},{5,7},{6,4},{7,5},{8,10},{9,11},{10,... | collective-permute-start | bytes 1572872 | tf_op jit(solution)/shard_map/ppermute | solution.py:303
  28.5 18.1 %collective-permute-start.10 = (bf16[2,128,512]{2,1,0:T(8,128)(2,1)S(1)}, bf16[2,128,512]{2,1,0:T(8,128)(2,1)S(1)}, u32[]{:S(2)}, u32[]{:S(2)}) collective-permute-start(bf16[2,128,512]{2,1,0:T(8,128)(2,1)S(1)} %get-tuple-element.41), channel_id=1, source_target_pairs={{0,1},{1,2},{2,3},{3,0},{4,5},{5,6},{6,7},{7,4},{8,9},{9,10},{10,1... | collective-permute-start | bytes 786440 | tf_op jit(solution)/shard_map/ppermute | solution.py:303
  30.1 18.3 %collective-permute-start.11 = (bf16[2,128,512]{2,1,0:T(8,128)(2,1)S(1)}, bf16[2,128,512]{2,1,0:T(8,128)(2,1)S(1)}, u32[]{:S(2)}, u32[]{:S(2)}) collective-permute-start(bf16[2,128,512]{2,1,0:T(8,128)(2,1)S(1)} %get-tuple-element.42), channel_id=1, source_target_pairs={{0,3},{1,0},{2,1},{3,2},{4,7},{5,4},{6,5},{7,6},{8,11},{9,8},{10,9... | collective-permute-start | bytes 786440 | tf_op jit(solution)/shard_map/ppermute | solution.py:303
  31.8 16.6 %collective-permute-start.12 = (bf16[2,128,512]{2,1,0:T(8,128)(2,1)S(1)}, bf16[2,128,512]{2,1,0:T(8,128)(2,1)S(1)}, u32[]{:S(2)}, u32[]{:S(2)}) collective-permute-start(bf16[2,128,512]{2,1,0:T(8,128)(2,1)S(1)} %get-tuple-element.43), channel_id=1, source_target_pairs={{0,2},{1,3},{2,0},{3,1},{4,6},{5,7},{6,4},{7,5},{8,10},{9,11},{10,... | collective-permute-start | bytes 786440 | tf_op jit(solution)/shard_map/ppermute | solution.py:303
  32.4 6.6 %copy-start.5 = (bf16[2,128,1024]{2,1,0:T(8,128)(2,1)S(1)}, bf16[2,128,1024]{2,1,0:T(8,128)(2,1)}, u32[]{:S(2)}) copy-start(bf16[2,128,1024]{2,1,0:T(8,128)(2,1)} %get-tuple-element.33.refs_4_) | copy-start | bytes 1572868
  35.0 25.7 %collective-permute-start.1 = (bf16[2,128,512]{2,1,0:T(8,128)(2,1)S(1)}, bf16[2,128,512]{2,1,0:T(8,128)(2,1)S(1)}, u32[]{:S(2)}, u32[]{:S(2)}) collective-permute-start(bf16[2,128,512]{2,1,0:T(8,128)(2,1)S(1)} %get-tuple-element.29), channel_id=1, source_target_pairs={{0,1},{1,2},{2,3},{3,0},{4,5},{5,6},{6,7},{7,4},{8,9},{9,10},{10,1... | collective-permute-start | bytes 786440 | tf_op jit(solution)/shard_map/ppermute | solution.py:303
  37.1 23.5 %collective-permute-start.2 = (bf16[2,128,512]{2,1,0:T(8,128)(2,1)S(1)}, bf16[2,128,512]{2,1,0:T(8,128)(2,1)S(1)}, u32[]{:S(2)}, u32[]{:S(2)}) collective-permute-start(bf16[2,128,512]{2,1,0:T(8,128)(2,1)S(1)} %get-tuple-element.30), channel_id=1, source_target_pairs={{0,3},{1,0},{2,1},{3,2},{4,7},{5,4},{6,5},{7,6},{8,11},{9,8},{10,9... | collective-permute-start | bytes 786440 | tf_op jit(solution)/shard_map/ppermute | solution.py:303
  46.6 14.1 %collective-permute-start.9 = (bf16[2,128,512]{2,1,0:T(8,128)(2,1)S(1)}, bf16[2,128,512]{2,1,0:T(8,128)(2,1)S(1)}, u32[]{:S(2)}, u32[]{:S(2)}) collective-permute-start(bf16[2,128,512]{2,1,0:T(8,128)(2,1)S(1)} %cut_2.3), channel_id=1, source_target_pairs={{0,2},{1,3},{2,0},{3,1},{4,6},{5,7},{6,4},{7,5},{8,10},{9,11},{10,... | collective-permute-start | bytes 786440 | tf_op jit(solution)/shard_map/ppermute | solution.py:303
  53.3 18.4 %collective-permute-start.13 = (bf16[2,512,128]{2,1,0:T(8,128)(2,1)S(1)}, bf16[2,512,128]{2,1,0:T(8,128)(2,1)S(1)}, u32[]{:S(2)}, u32[]{:S(2)}) collective-permute-start(bf16[2,512,128]{2,1,0:T(8,128)(2,1)S(1)} %get-tuple-element.50), channel_id=1, source_target_pairs={{4,0},{8,4},{12,8},{16,12},{20,16},{24,20},{28,24},{32,28},{36,32}... | collective-permute-start | bytes 786440 | tf_op jit(solution)/shard_map/ppermute | solution.py:298
  65.7 9.9 %collective-permute-start.14 = (bf16[2,512,128]{2,1,0:T(8,128)(2,1)S(1)}, bf16[2,512,128]{2,1,0:T(8,128)(2,1)S(1)}, u32[]{:S(2)}, u32[]{:S(2)}) collective-permute-start(bf16[2,512,128]{2,1,0:T(8,128)(2,1)S(1)} %get-tuple-element.52), channel_id=1, source_target_pairs={{4,0},{8,4},{12,8},{16,12},{20,16},{24,20},{28,24},{32,28},{36,32}... | collective-permute-start | bytes 786440 | tf_op jit(solution)/shard_map/ppermute | solution.py:298

commit v3 on v2

--- a/solution.py
+++ b/solution.py
@@ -342,8 +342,8 @@
     *sent_c, own_c = cut_heads(2, (1, -1, 0), got_a[:1])
     pieces = [[*got_a, own_a], [*around(sent_b), own_b]]
 
-    query_grad, sums, passed = None, None, []
-    total, prior = [], []
+    query_grad, sums, kept = None, None, []
+    total = []
     for at, part in enumerate(PARTS):
         ends = at + 1 == len(PARTS) or PARTS[at + 1][0] != part[0]
         query_grad, sums, *more = attention(
@@ -355,18 +355,19 @@
             query_grad,
             sums,
             ends,
-            passed,
+            kept if at + 1 == len(PARTS) else [],
         )
         if at == 0:
             sent_c += cut_heads(2, (2,), more)
             pieces.append([*around(sent_c), own_c])
-        if passed:
-            prior.append(from_behind(more.pop(), "cp", -1))
-        passed = []
         if ends:
             total.append(sums[:, length:, :])
-            passed = more
             sums = None
+            if at + 1 < len(PARTS):
+                kept = more
+            else:
+                prior = [from_behind(more.pop(), "cp", -1)]
+                passed = more
     prior.append(from_behind(passed[0], "cp", -1))
     scale = 1.0 / math.sqrt(HEAD_DIM)
     key_grad, value_grad = [

time: 77.4 us -> 85.6 us (1.11)
  the two profiles are of different devices: /device:TPU:24 before, /device:TPU:22 now
where the time goes in v3:
time: 85.6 us; the launch traced here: 85.2 us
  starting transfers between devices  28.7 us (34%)
  waiting for transfers between devices  27.5 us (32%)
  Pallas kernels  23 us (27%)
  local copies, waits for them, and re-layouts  2.3 us (3%)
  other arithmetic  2.24 us (3%)
  between operations  1.43 us (2%)
    pallas_call x3, Pallas kernels, attention(): pl.pallas_call(functools.partial(attention_kernel, part, sums is None, en...  19.3 us
    ppermute x12, waiting for transfers between devices, around(): lax.ppermute(piece, 'hd', [(i, (i + shift) % 4) for i in range(4)])  17.4 us
    ppermute x12, starting transfers between devices, around(): lax.ppermute(piece, 'hd', [(i, (i + shift) % 4) for i in range(4)])  15.7 us
    ppermute x3, starting transfers between devices, from_behind(): return lax.ppermute(shard, axis, pairs)  13 us
    ppermute x3, waiting for transfers between devices, from_behind(): return lax.ppermute(shard, axis, pairs)  10.1 us
    pallas_call x1, Pallas kernels, open_cut(): pl.pallas_call(open_kernel, out_shape=tuple(shapes), in_specs=[SMEM] + [A...  3.08 us
  transfers between devices with their start and end apart: 15, of which 7 were waited for; matrix products, arithmetic and copies ran while one was open for 2% of the time, Pallas kernels for 17%

profile of v3, /device:TPU:22, one launch (start us, length us, event | category | flops | bytes accessed | tf_op | source)
XLA Modules:
  0.0 85.2 jit_solution(11370002712388352890)
XLA Ops:
  0.7 3.1 %open_cut.1 = (bf16[2,128,256]{2,1,0:T(8,128)(2,1)}, bf16[2,128,256]{2,1,0:T(8,128)(2,1)}, bf16[2,128,256]{2,1,0:T(8,128)(2,1)}, bf16[2,128,1024]{2,1,0:T(8,128)...) custom-call(s32[1]{0:T(128)} %bitcast.me_ref, bf16[128,1024]{1,0:T(8,128)(2,1)} %left.7, ...), custom_call_target="tpu_custom_call" | custom-call | bytes 4194304 | tf_op jit(solution)/shard_map/open_cut/pallas_call | solution.py:86
  3.8 0.6 collective-permute-start.4
  4.3 1.5 %collective-permute-start.6 = (bf16[2,128,256]{2,1,0:T(8,128)(2,1)}, bf16[2,128,256]{2,1,0:T(8,128)(2,1)S(1)}, u32[]{:S(2)}, u32[]{:S(2)}) collective-permute-start(bf16[2,128,256]{2,1,0:T(8,128)(2,1)} %get-tuple-element.34), channel_id=1, source_target_pairs={{0,3},{1,0},{2,1},{3,2},{4,7},{5,4},{6,5},{7,6},{8,11},{9,8},{10,9... | collective-permute-start | bytes 393224 | tf_op jit(solution)/shard_map/ppermute | solution.py:303
  5.9 1.4 %collective-permute-start.7 = (bf16[2,128,256]{2,1,0:T(8,128)(2,1)}, bf16[2,128,256]{2,1,0:T(8,128)(2,1)S(1)}, u32[]{:S(2)}, u32[]{:S(2)}) collective-permute-start(bf16[2,128,256]{2,1,0:T(8,128)(2,1)} %get-tuple-element.35), channel_id=1, source_target_pairs={{0,2},{1,3},{2,0},{3,1},{4,6},{5,7},{6,4},{7,5},{8,10},{9,11},{10,... | collective-permute-start | bytes 393224 | tf_op jit(solution)/shard_map/ppermute | solution.py:303
  7.3 2.1 %collective-permute-start = (bf16[2,128,1024]{2,1,0:T(8,128)(2,1)}, bf16[2,128,1024]{2,1,0:T(8,128)(2,1)}, u32[]{:S(2)}, u32[]{:S(2)}) collective-permute-start(bf16[2,128,1024]{2,1,0:T(8,128)(2,1)} %get-tuple-element.28), channel_id=1, source_target_pairs={{0,1},{1,2},{2,3},{3,0},{4,5},{5,6},{6,7},{7,4},{8,9},{9,10},{10,1... | collective-permute-start | bytes 1572872 | tf_op jit(solution)/shard_map/ppermute | solution.py:303
  9.4 0.0 collective-permute-start.3
  9.4 0.6 dynamic_slice.10
  10.5 0.8 dynamic-slice_select_fusion
  11.3 0.4 convert_reduce_fusion
  11.7 0.0 collective-permute-done.4.refs_0_.got_a
  11.7 1.4 %collective-permute-done.6.got_b = bf16[2,128,256]{2,1,0:T(8,128)(2,1)S(1)} collective-permute-done((bf16[2,128,256]{2,1,0:T(8,128)(2,1)}, bf16[2,128,256]{2,1,0:T(8,128)(2,1)S(1)}, u32[]{:S(2)}, u32[]{:S(2)}) %collective-permute-start.6) | collective-permute-done | bytes 131104 | tf_op jit(solution)/shard_map/ppermute | solution.py:303
  13.1 1.2 %collective-permute-done.7.got_c = bf16[2,128,256]{2,1,0:T(8,128)(2,1)S(1)} collective-permute-done((bf16[2,128,256]{2,1,0:T(8,128)(2,1)}, bf16[2,128,256]{2,1,0:T(8,128)(2,1)S(1)}, u32[]{:S(2)}, u32[]{:S(2)}) %collective-permute-start.7) | collective-permute-done | bytes 131104 | tf_op jit(solution)/shard_map/ppermute | solution.py:303
  14.3 0.1 join.1.kv_own
  14.4 1.9 %collective-permute-start.8 = (bf16[2,512,256]{2,1,0:T(8,128)(2,1)S(1)}, bf16[2,512,256]{2,1,0:T(8,128)(2,1)S(1)}, u32[]{:S(2)}, u32[]{:S(2)}) collective-permute-start(bf16[2,512,256]{2,1,0:T(8,128)(2,1)S(1)} %join.1.kv_own), channel_id=1, source_target_pairs={{0,4},{4,8},{8,12},{12,16},{16,20},{20,24},{24,28},{28,32},{32,36}... | collective-permute-start | bytes 1572872 | tf_op jit(solution)/shard_map/ppermute | solution.py:298
  16.3 0.1 slice.33
  16.4 1.6 %copy-done.1 = bf16[128,8192]{1,0:T(8,128)(2,1)S(1)} copy-done((bf16[128,8192]{1,0:T(8,128)(2,1)S(1)}, bf16[128,8192]{1,0:T(8,128)(2,1)}, u32[]{:S(2)}) %copy-start.1) | copy-done | bytes 2097176
  18.0 2.6 %collective-permute-start.5 = (bf16[2,128,1024]{2,1,0:T(8,128)(2,1)S(1)}, bf16[2,128,1024]{2,1,0:T(8,128)(2,1)S(1)}, u32[]{:S(2)}, u32[]{:S(2)}) collective-permute-start(bf16[2,128,1024]{2,1,0:T(8,128)(2,1)S(1)} %cut_0.1), channel_id=1, source_target_pairs={{0,2},{1,3},{2,0},{3,1},{4,6},{5,7},{6,4},{7,5},{8,10},{9,11},{10,... | collective-permute-start | bytes 1572872 | tf_op jit(solution)/shard_map/ppermute | solution.py:303
  20.7 6.3 %collective-permute-done.8.kv_prev = bf16[2,512,256]{2,1,0:T(8,128)(2,1)S(1)} collective-permute-done((bf16[2,512,256]{2,1,0:T(8,128)(2,1)S(1)}, bf16[2,512,256]{2,1,0:T(8,128)(2,1)S(1)}, u32[]{:S(2)}, u32[]{:S(2)}) %collective-permute-start.8) | collective-permute-done | bytes 524320 | tf_op jit(solution)/shard_map/ppermute | solution.py:298
  27.0 0.4 prepare.1
  27.3 0.0 copy-done.2
  27.4 0.1 cut_1.1
  27.5 1.5 %collective-permute-start.10 = (bf16[2,128,512]{2,1,0:T(8,128)(2,1)S(1)}, bf16[2,128,512]{2,1,0:T(8,128)(2,1)S(1)}, u32[]{:S(2)}, u32[]{:S(2)}) collective-permute-start(bf16[2,128,512]{2,1,0:T(8,128)(2,1)S(1)} %get-tuple-element.41), channel_id=1, source_target_pairs={{0,1},{1,2},{2,3},{3,0},{4,5},{5,6},{6,7},{7,4},{8,9},{9,10},{10,1... | collective-permute-start | bytes 786440 | tf_op jit(solution)/shard_map/ppermute | solution.py:303
  29.0 0.1 pad_add_fusion.1.refs_0_
  29.1 0.0 collective-permute-done.refs_0_.refs_1_
  29.1 0.1 cut_2.2
  29.1 1.7 %collective-permute-start.1 = (bf16[2,128,512]{2,1,0:T(8,128)(2,1)S(1)}, bf16[2,128,512]{2,1,0:T(8,128)(2,1)S(1)}, u32[]{:S(2)}, u32[]{:S(2)}) collective-permute-start(bf16[2,128,512]{2,1,0:T(8,128)(2,1)S(1)} %get-tuple-element.29), channel_id=1, source_target_pairs={{0,1},{1,2},{2,3},{3,0},{4,5},{5,6},{6,7},{7,4},{8,9},{9,10},{10,1... | collective-permute-start | bytes 786440 | tf_op jit(solution)/shard_map/ppermute | solution.py:303
  30.8 0.4 collective-permute-start.2
  31.2 5.0 %collective-permute-done.3.refs_2_ = bf16[2,128,1024]{2,1,0:T(8,128)(2,1)} collective-permute-done((bf16[2,128,1024]{2,1,0:T(8,128)(2,1)}, bf16[2,128,1024]{2,1,0:T(8,128)(2,1)}, u32[]{:S(2)}, u32[]{:S(2)}) %collective-permute-start.3) | collective-permute-done | bytes 524320 | tf_op jit(solution)/shard_map/ppermute | solution.py:303
  36.2 0.0 collective-permute-start.11
  36.2 0.0 collective-permute-done.5.refs_3_
  36.2 1.5 %collective-permute-start.12 = (bf16[2,128,512]{2,1,0:T(8,128)(2,1)S(1)}, bf16[2,128,512]{2,1,0:T(8,128)(2,1)S(1)}, u32[]{:S(2)}, u32[]{:S(2)}) collective-permute-start(bf16[2,128,512]{2,1,0:T(8,128)(2,1)S(1)} %get-tuple-element.43), channel_id=1, source_target_pairs={{0,2},{1,3},{2,0},{3,1},{4,6},{5,7},{6,4},{7,5},{8,10},{9,11},{10,... | collective-permute-start | bytes 786440 | tf_op jit(solution)/shard_map/ppermute | solution.py:303
  37.7 8.5 %attend_0.1 = (bf16[512,2048]{1,0:T(8,128)(2,1)}, f32[2,1024,128]{2,1,0:T(8,128)S(1)}, bf16[2,512,128]{2,1,0:T(8,128)(2,1)S(1)}) custom-call(s32[5]{0:T(128)S(1)} %pad_add_fusion.1.refs_0_, bf16[2,128,1024]{2,1,0:T(8,128)(2,1)} %collective-permute-done.refs_0_.refs_1_, bf16[2,128,1024]{2,1,0:T(8,128)(2,1)} %collective-permute-done.3.refs_2_, ...), custom_call_target="tpu_custom_call" | custom-call | flops 1677721600 | bytes 3145728 | tf_op jit(solution)/shard_map/attend_0/pallas_call | solution.py:273
  46.2 0.0 collective-permute-done.10.refs_1_
  46.3 2.4 %collective-permute-start.9 = (bf16[2,128,512]{2,1,0:T(8,128)(2,1)S(1)}, bf16[2,128,512]{2,1,0:T(8,128)(2,1)S(1)}, u32[]{:S(2)}, u32[]{:S(2)}) collective-permute-start(bf16[2,128,512]{2,1,0:T(8,128)(2,1)S(1)} %cut_2.3), channel_id=1, source_target_pairs={{0,2},{1,3},{2,0},{3,1},{4,6},{5,7},{6,4},{7,5},{8,10},{9,11},{10,... | collective-permute-start | bytes 786440 | tf_op jit(solution)/shard_map/ppermute | solution.py:303
  48.6 9.8 %collective-permute-done.11.refs_2_ = bf16[2,128,512]{2,1,0:T(8,128)(2,1)S(1)} collective-permute-done((bf16[2,128,512]{2,1,0:T(8,128)(2,1)S(1)}, bf16[2,128,512]{2,1,0:T(8,128)(2,1)S(1)}, u32[]{:S(2)}, u32[]{:S(2)}) %collective-permute-start.11) | collective-permute-done | bytes 262176 | tf_op jit(solution)/shard_map/ppermute | solution.py:303
  58.5 0.0 collective-permute-done.12.refs_3_
  58.5 5.4 %attend_1.1 = (bf16[512,2048]{1,0:T(8,128)(2,1)}, f32[2,1024,128]{2,1,0:T(8,128)S(1)}) custom-call(s32[5]{0:T(128)S(1)} %pad_add_fusion.1.refs_0_, bf16[2,128,512]{2,1,0:T(8,128)(2,1)S(1)} %collective-permute-done.10.refs_1_, bf16[2,128,512]{2,1,0:T(8,128)(2,1)S(1)} %collective-permute-done.11.refs_2_, ...), custom_call_target="tpu_custom_call", output_to_operand_aliasing={{0}: (8, {})} | custom-call | flops 838860800 | bytes 1572864 | tf_op jit(solution)/shard_map/attend_1/pallas_call | solution.py:273
  63.8 0.0 collective-permute-done.1.refs_1_
  63.9 0.0 collective-permute-done.2.refs_2_
  63.9 0.0 collective-permute-done.9.refs_3_
  63.9 5.4 %attend_2.1 = (bf16[512,2048]{1,0:T(8,128)(2,1)}, f32[2,1024,128]{2,1,0:T(8,128)S(1)}, bf16[2,512,128]{2,1,0:T(8,128)(2,1)S(1)}, bf16[2,512,128]{2,1,0:T(8,128)(2,1)S(1)}) custom-call(s32[5]{0:T(128)S(1)} %pad_add_fusion.1.refs_0_, bf16[2,128,512]{2,1,0:T(8,128)(2,1)S(1)} %collective-permute-done.1.refs_1_, ...), custom_call_target="tpu_custom_call", output_to_operand_aliasing={{0}: (8, {}), {3}: (10, {})} | custom-call | flops 838860800 | bytes 1572864 | tf_op jit(solution)/shard_map/attend_2/pallas_call | solution.py:273
  69.3 8.2 %collective-permute-start.13 = (bf16[2,512,128]{2,1,0:T(8,128)(2,1)S(1)}, bf16[2,512,128]{2,1,0:T(8,128)(2,1)S(1)}, u32[]{:S(2)}, u32[]{:S(2)}) collective-permute-start(bf16[2,512,128]{2,1,0:T(8,128)(2,1)S(1)} %get-tuple-element.50), channel_id=1, source_target_pairs={{4,0},{8,4},{12,8},{16,12},{20,16},{24,20},{28,24},{32,28},{36,32}... | collective-permute-start | bytes 786440 | tf_op jit(solution)/shard_map/ppermute | solution.py:298
  77.4 2.9 %collective-permute-start.14 = (bf16[2,512,128]{2,1,0:T(8,128)(2,1)S(1)}, bf16[2,512,128]{2,1,0:T(8,128)(2,1)S(1)}, u32[]{:S(2)}, u32[]{:S(2)}) collective-permute-start(bf16[2,512,128]{2,1,0:T(8,128)(2,1)S(1)} %get-tuple-element.52), channel_id=1, source_target_pairs={{4,0},{8,4},{12,8},{16,12},{20,16},{24,20},{28,24},{32,28},{36,32}... | collective-permute-start | bytes 786440 | tf_op jit(solution)/shard_map/ppermute | solution.py:298
  80.4 0.9 %collective-permute-done.13 = bf16[2,512,128]{2,1,0:T(8,128)(2,1)S(1)} collective-permute-done((bf16[2,512,128]{2,1,0:T(8,128)(2,1)S(1)}, bf16[2,512,128]{2,1,0:T(8,128)(2,1)S(1)}, u32[]{:S(2)}, u32[]{:S(2)}) %collective-permute-start.13) | collective-permute-done | bytes 262176 | tf_op jit(solution)/shard_map/ppermute | solution.py:298
  81.3 0.1 fusion.2
  81.4 2.9 %collective-permute-done.14 = bf16[2,512,128]{2,1,0:T(8,128)(2,1)S(1)} collective-permute-done((bf16[2,512,128]{2,1,0:T(8,128)(2,1)S(1)}, bf16[2,512,128]{2,1,0:T(8,128)(2,1)S(1)}, u32[]{:S(2)}, u32[]{:S(2)}) %collective-permute-start.14) | collective-permute-done | bytes 262176 | tf_op jit(solution)/shard_map/ppermute | solution.py:298
  84.3 0.1 fusion.3
  84.3 0.8 pad_maximum_fusion
  (18 shorter events, 0.1 us)
Async XLA Ops:
  0.6 8.7 %copy-start.6 = (s32[64]{0:T(128)S(1)}, s32[64]{0:T(128)}, u32[]{:S(2)}) copy-start(s32[64]{0:T(128)} %param.11) | copy-start | bytes 772
  0.6 13.7 %copy-start.3 = (bf16[128,1024]{1,0:T(8,128)(2,1)S(1)}, bf16[128,1024]{1,0:T(8,128)(2,1)}, u32[]{:S(2)}) copy-start(bf16[128,1024]{1,0:T(8,128)(2,1)} %left.7) | copy-start | bytes 786436
  0.7 13.6 %copy-start.4 = (bf16[128,1024]{1,0:T(8,128)(2,1)S(1)}, bf16[128,1024]{1,0:T(8,128)(2,1)}, u32[]{:S(2)}) copy-start(bf16[128,1024]{1,0:T(8,128)(2,1)} %right.7) | copy-start | bytes 786436
  0.7 15.7 %copy-start = (bf16[128,8192]{1,0:T(8,128)(2,1)S(1)}, bf16[128,8192]{1,0:T(8,128)(2,1)}, u32[]{:S(2)}) copy-start(bf16[128,8192]{1,0:T(8,128)(2,1)} %left.9) | copy-start | bytes 6291460
  3.8 7.9 %collective-permute-start.4 = (bf16[2,128,256]{2,1,0:T(8,128)(2,1)}, bf16[2,128,256]{2,1,0:T(8,128)(2,1)S(1)}, u32[]{:S(2)}, u32[]{:S(2)}) collective-permute-start(bf16[2,128,256]{2,1,0:T(8,128)(2,1)} %get-tuple-element.32), channel_id=1, source_target_pairs={{0,1},{1,2},{2,3},{3,0},{4,5},{5,6},{6,7},{7,4},{8,9},{9,10},{10,1... | collective-permute-start | bytes 393224 | tf_op jit(solution)/shard_map/ppermute | solution.py:303
  4.3 8.7 %collective-permute-start.6 = (bf16[2,128,256]{2,1,0:T(8,128)(2,1)}, bf16[2,128,256]{2,1,0:T(8,128)(2,1)S(1)}, u32[]{:S(2)}, u32[]{:S(2)}) collective-permute-start(bf16[2,128,256]{2,1,0:T(8,128)(2,1)} %get-tuple-element.34), channel_id=1, source_target_pairs={{0,3},{1,0},{2,1},{3,2},{4,7},{5,4},{6,5},{7,6},{8,11},{9,8},{10,9... | collective-permute-start | bytes 393224 | tf_op jit(solution)/shard_map/ppermute | solution.py:303
  5.9 8.4 %collective-permute-start.7 = (bf16[2,128,256]{2,1,0:T(8,128)(2,1)}, bf16[2,128,256]{2,1,0:T(8,128)(2,1)S(1)}, u32[]{:S(2)}, u32[]{:S(2)}) collective-permute-start(bf16[2,128,256]{2,1,0:T(8,128)(2,1)} %get-tuple-element.35), channel_id=1, source_target_pairs={{0,2},{1,3},{2,0},{3,1},{4,6},{5,7},{6,4},{7,5},{8,10},{9,11},{10,... | collective-permute-start | bytes 393224 | tf_op jit(solution)/shard_map/ppermute | solution.py:303
  7.3 21.8 %collective-permute-start = (bf16[2,128,1024]{2,1,0:T(8,128)(2,1)}, bf16[2,128,1024]{2,1,0:T(8,128)(2,1)}, u32[]{:S(2)}, u32[]{:S(2)}) collective-permute-start(bf16[2,128,1024]{2,1,0:T(8,128)(2,1)} %get-tuple-element.28), channel_id=1, source_target_pairs={{0,1},{1,2},{2,3},{3,0},{4,5},{5,6},{6,7},{7,4},{8,9},{9,10},{10,1... | collective-permute-start | bytes 1572872 | tf_op jit(solution)/shard_map/ppermute | solution.py:303
  9.4 26.8 %collective-permute-start.3 = (bf16[2,128,1024]{2,1,0:T(8,128)(2,1)}, bf16[2,128,1024]{2,1,0:T(8,128)(2,1)}, u32[]{:S(2)}, u32[]{:S(2)}) collective-permute-start(bf16[2,128,1024]{2,1,0:T(8,128)(2,1)} %get-tuple-element.31), channel_id=1, source_target_pairs={{0,3},{1,0},{2,1},{3,2},{4,7},{5,4},{6,5},{7,6},{8,11},{9,8},{10,9... | collective-permute-start | bytes 1572872 | tf_op jit(solution)/shard_map/ppermute | solution.py:303
  14.4 12.6 %collective-permute-start.8 = (bf16[2,512,256]{2,1,0:T(8,128)(2,1)S(1)}, bf16[2,512,256]{2,1,0:T(8,128)(2,1)S(1)}, u32[]{:S(2)}, u32[]{:S(2)}) collective-permute-start(bf16[2,512,256]{2,1,0:T(8,128)(2,1)S(1)} %join.1.kv_own), channel_id=1, source_target_pairs={{0,4},{4,8},{8,12},{12,16},{16,20},{20,24},{24,28},{28,32},{32,36}... | collective-permute-start | bytes 1572872 | tf_op jit(solution)/shard_map/ppermute | solution.py:298
  16.4 1.6 %copy-start.1 = (bf16[128,8192]{1,0:T(8,128)(2,1)S(1)}, bf16[128,8192]{1,0:T(8,128)(2,1)}, u32[]{:S(2)}) copy-start(bf16[128,8192]{1,0:T(8,128)(2,1)} %right.9) | copy-start | bytes 6291460
  18.0 9.4 %copy-start.2 = (bf16[128,8192]{1,0:T(8,128)(2,1)S(1)}, bf16[128,8192]{1,0:T(8,128)(2,1)}, u32[]{:S(2)}) copy-start(bf16[128,8192]{1,0:T(8,128)(2,1)} %right.9) | copy-start | bytes 6291460
  18.0 18.2 %collective-permute-start.5 = (bf16[2,128,1024]{2,1,0:T(8,128)(2,1)S(1)}, bf16[2,128,1024]{2,1,0:T(8,128)(2,1)S(1)}, u32[]{:S(2)}, u32[]{:S(2)}) collective-permute-start(bf16[2,128,1024]{2,1,0:T(8,128)(2,1)S(1)} %cut_0.1), channel_id=1, source_target_pairs={{0,2},{1,3},{2,0},{3,1},{4,6},{5,7},{6,4},{7,5},{8,10},{9,11},{10,... | collective-permute-start | bytes 1572872 | tf_op jit(solution)/shard_map/ppermute | solution.py:303
  27.5 18.8 %collective-permute-start.10 = (bf16[2,128,512]{2,1,0:T(8,128)(2,1)S(1)}, bf16[2,128,512]{2,1,0:T(8,128)(2,1)S(1)}, u32[]{:S(2)}, u32[]{:S(2)}) collective-permute-start(bf16[2,128,512]{2,1,0:T(8,128)(2,1)S(1)} %get-tuple-element.41), channel_id=1, source_target_pairs={{0,1},{1,2},{2,3},{3,0},{4,5},{5,6},{6,7},{7,4},{8,9},{9,10},{10,1... | collective-permute-start | bytes 786440 | tf_op jit(solution)/shard_map/ppermute | solution.py:303
  29.1 8.6 %copy-start.5 = (bf16[2,128,1024]{2,1,0:T(8,128)(2,1)S(1)}, bf16[2,128,1024]{2,1,0:T(8,128)(2,1)}, u32[]{:S(2)}) copy-start(bf16[2,128,1024]{2,1,0:T(8,128)(2,1)} %get-tuple-element.33.refs_4_) | copy-start | bytes 1572868
  29.1 34.7 %collective-permute-start.1 = (bf16[2,128,512]{2,1,0:T(8,128)(2,1)S(1)}, bf16[2,128,512]{2,1,0:T(8,128)(2,1)S(1)}, u32[]{:S(2)}, u32[]{:S(2)}) collective-permute-start(bf16[2,128,512]{2,1,0:T(8,128)(2,1)S(1)} %get-tuple-element.29), channel_id=1, source_target_pairs={{0,1},{1,2},{2,3},{3,0},{4,5},{5,6},{6,7},{7,4},{8,9},{9,10},{10,1... | collective-permute-start | bytes 786440 | tf_op jit(solution)/shard_map/ppermute | solution.py:303
  30.8 33.0 %collective-permute-start.2 = (bf16[2,128,512]{2,1,0:T(8,128)(2,1)S(1)}, bf16[2,128,512]{2,1,0:T(8,128)(2,1)S(1)}, u32[]{:S(2)}, u32[]{:S(2)}) collective-permute-start(bf16[2,128,512]{2,1,0:T(8,128)(2,1)S(1)} %get-tuple-element.30), channel_id=1, source_target_pairs={{0,3},{1,0},{2,1},{3,2},{4,7},{5,4},{6,5},{7,6},{8,11},{9,8},{10,9... | collective-permute-start | bytes 786440 | tf_op jit(solution)/shard_map/ppermute | solution.py:303
  36.2 22.2 %collective-permute-start.11 = (bf16[2,128,512]{2,1,0:T(8,128)(2,1)S(1)}, bf16[2,128,512]{2,1,0:T(8,128)(2,1)S(1)}, u32[]{:S(2)}, u32[]{:S(2)}) collective-permute-start(bf16[2,128,512]{2,1,0:T(8,128)(2,1)S(1)} %get-tuple-element.42), channel_id=1, source_target_pairs={{0,3},{1,0},{2,1},{3,2},{4,7},{5,4},{6,5},{7,6},{8,11},{9,8},{10,9... | collective-permute-start | bytes 786440 | tf_op jit(solution)/shard_map/ppermute | solution.py:303
  36.2 22.2 %collective-permute-start.12 = (bf16[2,128,512]{2,1,0:T(8,128)(2,1)S(1)}, bf16[2,128,512]{2,1,0:T(8,128)(2,1)S(1)}, u32[]{:S(2)}, u32[]{:S(2)}) collective-permute-start(bf16[2,128,512]{2,1,0:T(8,128)(2,1)S(1)} %get-tuple-element.43), channel_id=1, source_target_pairs={{0,2},{1,3},{2,0},{3,1},{4,6},{5,7},{6,4},{7,5},{8,10},{9,11},{10,... | collective-permute-start | bytes 786440 | tf_op jit(solution)/shard_map/ppermute | solution.py:303
  46.3 17.6 %collective-permute-start.9 = (bf16[2,128,512]{2,1,0:T(8,128)(2,1)S(1)}, bf16[2,128,512]{2,1,0:T(8,128)(2,1)S(1)}, u32[]{:S(2)}, u32[]{:S(2)}) collective-permute-start(bf16[2,128,512]{2,1,0:T(8,128)(2,1)S(1)} %cut_2.3), channel_id=1, source_target_pairs={{0,2},{1,3},{2,0},{3,1},{4,6},{5,7},{6,4},{7,5},{8,10},{9,11},{10,... | collective-permute-start | bytes 786440 | tf_op jit(solution)/shard_map/ppermute | solution.py:303
  69.3 12.1 %collective-permute-start.13 = (bf16[2,512,128]{2,1,0:T(8,128)(2,1)S(1)}, bf16[2,512,128]{2,1,0:T(8,128)(2,1)S(1)}, u32[]{:S(2)}, u32[]{:S(2)}) collective-permute-start(bf16[2,512,128]{2,1,0:T(8,128)(2,1)S(1)} %get-tuple-element.50), channel_id=1, source_target_pairs={{4,0},{8,4},{12,8},{16,12},{20,16},{24,20},{28,24},{32,28},{36,32}... | collective-permute-start | bytes 786440 | tf_op jit(solution)/shard_map/ppermute | solution.py:298
  77.4 6.8 %collective-permute-start.14 = (bf16[2,512,128]{2,1,0:T(8,128)(2,1)S(1)}, bf16[2,512,128]{2,1,0:T(8,128)(2,1)S(1)}, u32[]{:S(2)}, u32[]{:S(2)}) collective-permute-start(bf16[2,512,128]{2,1,0:T(8,128)(2,1)S(1)} %get-tuple-element.52), channel_id=1, source_target_pairs={{4,0},{8,4},{12,8},{16,12},{20,16},{24,20},{28,24},{32,28},{36,32}... | collective-permute-start | bytes 786440 | tf_op jit(solution)/shard_map/ppermute | solution.py:298
